TPU v7x, 256 devices: a whole 4x4x8 slice. The times are simulated.
256 devices in a mesh: param: 16 (over z_hi, y), sensor: 16 (over x, z_lo, core).
Axes of the slice: x: 4, y: 4, z: 8 (z_hi: 4, z_lo: 2; z = z_hi * 2 + z_lo), core: 2. Of those that a mesh axis runs over, the one named last changes fastest.
Arguments:
- seafloor_motion: float32 [420, 65536], P(None, ('param', 'sensor')), may hold values from -6 to 6
- response_blocks: bfloat16 [16, 2, 640, 65536], P(None, None, 'sensor', 'param'), may hold values from -0.25 to 0.25
- frequencies: int32 [16], replicated, may hold values from 0 to 210
- station_of_row: int32 [640], P('sensor'), may hold values from 0 to 639, each once
- noise_precision: float32 [640], replicated, may hold values from 0.2 to 2
Outputs:
- hessian_action: float32 [420, 65536], P(None, ('param', 'sensor'))
Inputs may be any that keep to these rules, and one draw needn't show every extreme that they name: `station_of_row`: each station appears in exactly one sensor row. `frequencies`: frequency numbers may repeat.
All inputs are finite; a program needn't handle non-finite values.
Results may differ from a plain program's by a relative error of at most 0.004.
Values may be sent and summed in bfloat16 or wider, within the bound.
No kernel may reach another device: no remote copies, remote signals or barrier semaphores. Data moves between devices by JAX's collectives and lax.ppermute only.
A program may use at most 64 MiB of HBM per device.

v0:
```python
import math

import jax
import jax.numpy as jnp
from jax import lax
from jax.sharding import PartitionSpec as P


def per_device(seafloor_motion, response_blocks, frequencies, station_of_row, noise_precision):
    highest = lax.Precision.HIGHEST
    num_steps = seafloor_motion.shape[0]
    steps = jnp.arange(num_steps, dtype=jnp.int32)
    phase = frequencies[:, None] * steps[None, :] % num_steps
    angle = phase.astype(jnp.float32) * (2.0 * math.pi / num_steps)
    scale = 1.0 / math.sqrt(num_steps)
    cosine_table = jnp.cos(angle) * scale
    sine_table = jnp.sin(angle) * scale
    spec_real = jnp.dot(cosine_table, seafloor_motion, precision=highest)
    spec_imag = -jnp.dot(sine_table, seafloor_motion, precision=highest)
    spectrum = jnp.stack([spec_real, spec_imag], axis=1).astype(jnp.bfloat16)
    real_block = response_blocks[:, 0]
    imag_block = response_blocks[:, 1]
    piece = lax.all_gather(spectrum, "sensor", axis=2, tiled=True)
    data_real = jnp.einsum(
        "ksp,kp->ks", real_block, piece[:, 0], preferred_element_type=jnp.float32
    ) - jnp.einsum("ksp,kp->ks", imag_block, piece[:, 1], preferred_element_type=jnp.float32)
    data_imag = jnp.einsum(
        "ksp,kp->ks", real_block, piece[:, 1], preferred_element_type=jnp.float32
    ) + jnp.einsum("ksp,kp->ks", imag_block, piece[:, 0], preferred_element_type=jnp.float32)
    data = jnp.stack([data_real, data_imag], axis=1)
    stations = noise_precision.shape[0]
    matches = station_of_row[:, None] == jnp.arange(stations, dtype=jnp.int32)[None, :]
    weight = jnp.sum(jnp.where(matches, noise_precision[None, :], 0.0), axis=1)
    summed = lax.psum(data, "param")
    weighted = (summed * weight[None, None, :]).astype(jnp.bfloat16)
    wdata_real = weighted[:, 0]
    wdata_imag = weighted[:, 1]
    adj_real = jnp.einsum(
        "ksp,ks->kp", real_block, wdata_real, preferred_element_type=jnp.float32
    ) + jnp.einsum("ksp,ks->kp", imag_block, wdata_imag, preferred_element_type=jnp.float32)
    adj_imag = jnp.einsum(
        "ksp,ks->kp", real_block, wdata_imag, preferred_element_type=jnp.float32
    ) - jnp.einsum("ksp,ks->kp", imag_block, wdata_real, preferred_element_type=jnp.float32)
    adjoint = jnp.stack([adj_real, adj_imag], axis=1)
    own_adjoint = lax.psum_scatter(adjoint, "sensor", scatter_dimension=2, tiled=True)
    return jnp.dot(cosine_table.T, own_adjoint[:, 0], precision=highest) - jnp.dot(
        sine_table.T, own_adjoint[:, 1], precision=highest
    )


def solution(mesh):
    in_specs = (
        P(None, ("param", "sensor")),
        P(None, None, "sensor", "param"),
        P(),
        P("sensor"),
        P(),
    )
    out_specs = P(None, ("param", "sensor"))
    return jax.shard_map(
        per_device, mesh=mesh, in_specs=in_specs, out_specs=out_specs, check_vma=False
    )
```

profile of v0, /device:TPU:1, one launch (start us, length us, event | category | flops | bytes accessed | tf_op | source)
XLA Modules:
  0.0 204.6 jit_solution(577054876188764249)
XLA Ops:
  6.5 0.0 copy-start
  6.5 0.0 reduce-scatter.2.cloned.1.call-start
  6.5 1.0 copy-done
  7.5 1.3 fusion.25
  8.8 1.5 fusion.26
  10.4 22.6 %all_gather.3 = bf16[16,2,4096]{2,0,1:T(8,128)(2,1)S(1)} all-gather(bf16[16,2,256]{2,0,1:T(8,128)(2,1)S(1)} %pad_maximum_fusion.1), channel_id=1, replica_groups=mesh['param'=16,'sensor'=16] {'sensor'}, dimensions={2}, use_global_device_ids=true | all-gather | bytes 278528 | tf_op jit(solution)/shard_map/all_gather | solution.py:23
  32.9 4.0 %fusion.6 = f32[16,1,40]{2,1,0:T(1,128)S(1)} fusion(bf16[16,2,40,4096]{3,2,1,0:T(8,128)(2,1)} %param.6, bf16[16,4096,1]{1,0,2:T(8,128)(2,1)S(1)} %get-tuple-element.6), kind=kOutput, calls=%fused_computation.6 | convolution fusion | flops 5242880 | bytes 5376512 | tf_op jit(solution)/shard_map/ksp,kp->ks/dot_general | solution.py:26
  36.9 4.0 %fusion.12 = f32[16,1,40]{2,1,0:T(1,128)S(1)} fusion(bf16[16,2,40,4096]{3,2,1,0:T(8,128)(2,1)} %param.6, bf16[16,4096,1]{1,0,2:T(8,128)(2,1)S(1)} %get-tuple-element.6), kind=kOutput, calls=%fused_computation.12 | convolution fusion | flops 5242880 | bytes 5376512 | tf_op jit(solution)/shard_map/ksp,kp->ks/dot_general | solution.py:27
  40.9 0.0 copy-done.1
  40.9 1.5 fusion.4
  42.4 1.5 fusion.14
  43.8 70.5 %psum.7 = f32[16,2,40]{2,0,1:T(8,128)S(1)} all-reduce(f32[16,2,40]{2,0,1:T(8,128)S(1)} %pad_maximum_fusion.2), channel_id=1, replica_groups=mesh['param'=16,'sensor'=16] {'param'}, use_global_device_ids=true, to_apply=%region_0.1 | all-reduce | flops 1280 | bytes 10240 | tf_op jit(solution)/shard_map/psum | solution.py:34
  114.4 0.0 copy-done.3
  114.4 0.0 copy-done.4
  114.4 0.2 select_reduce_fusion
  114.6 0.0 slice-start.1
  114.6 3.7 %fusion.10 = f32[16,1,4096]{2,1,0:T(1,128)S(1)} fusion(bf16[16,2,40,4096]{3,2,1,0:T(8,128)(2,1)} %param.6, bf16[16,40,1]{1,0,2:T(8,128)(2,1)S(1)} %get-tuple-element.8), kind=kOutput, calls=%fused_computation.10 | convolution fusion | flops 5242880 | bytes 5506304 | tf_op jit(solution)/shard_map/ksp,ks->kp/dot_general | solution.py:38
  118.3 0.0 copy-start.2
  118.3 3.7 %fusion = f32[16,1,4096]{2,1,0:T(1,128)S(1)} fusion(bf16[16,2,40,4096]{3,2,1,0:T(8,128)(2,1)} %param.6, bf16[16,40,1]{1,0,2:T(8,128)(2,1)S(1)} %get-tuple-element.8), kind=kOutput, calls=%fused_computation | convolution fusion | flops 5242880 | bytes 5506304 | tf_op jit(solution)/shard_map/ksp,ks->kp/dot_general | solution.py:43
  122.0 3.6 %fusion.2 = f32[16,1,4096]{2,1,0:T(1,128)S(1)} fusion(bf16[16,2,40,4096]{3,2,1,0:T(8,128)(2,1)} %param.6, bf16[16,40,1]{1,0,2:T(8,128)(2,1)S(1)} %get-tuple-element.7), kind=kOutput, calls=%fused_computation.2 | convolution fusion | flops 5242880 | bytes 5506304 | tf_op jit(solution)/shard_map/ksp,ks->kp/dot_general | solution.py:40
  125.6 0.0 slice-done
  125.6 0.0 slice-done.1
  125.6 0.0 slice-done.2
  125.6 1.2 fusion.8
  126.8 0.3 fusion.28
  127.1 0.3 fusion.27
  127.4 0.9 pad_maximum_fusion
  128.3 0.0 reduce-scatter.2.cloned.1.call-update
  128.3 65.7 %reduce-scatter.2.cloned.1.call-done = f32[16,2,256]{2,0,1:T(8,128)} async-done(((f32[16,2,4096]{2,0,1:T(8,128)}), f32[16,2,256]{2,0,1:T(8,128)}) %reduce-scatter.2.cloned.1.call-update) | async-done | bytes 32784 | tf_op jit(solution)/shard_map/reduce_scatter | solution.py:45
  194.1 0.0 copy-done.2
  194.1 1.4 fusion.38
  195.5 2.2 %convolution_subtract_fusion = f32[420,256]{1,0:T(8,128)} fusion(f32[420,256]{1,0:T(8,128)S(1)} %fusion.38, f32[16,2,256]{2,0,1:T(8,128)} %reduce-scatter.2.cloned.1.call-done, s32[16]{0:T(128)S(1)} %copy-done.2), kind=kOutput, calls=%fused_computation.24 | convolution fusion | flops 20818560 | bytes 876608 | tf_op jit(solution)/shard_map/dot_general | solution.py:46
  (12 shorter events, 0.1 us)
Async XLA Ops:
  6.5 1.0 copy-start
  6.5 187.5 %reduce-scatter.2.cloned.1.call-start = ((), (), s32[]{:S(2)}) async-start(), calls=%async_computation.1 | async-start | bytes 557056 | tf_op jit(solution)/shard_map/reduce_scatter | solution.py:45
  7.5 33.3 %copy-start.1 = (bf16[16,2,40,4096]{3,2,1,0:T(8,128)(2,1)S(1)}, bf16[16,2,40,4096]{3,2,1,0:T(8,128)(2,1)}, u32[]{:S(2)}) copy-start(bf16[16,2,40,4096]{3,2,1,0:T(8,128)(2,1)} %param.6) | copy-start | bytes 31457284
  36.9 77.5 %copy-start.3 = (f32[640]{0:T(1024)S(1)}, f32[640]{0:T(1024)}, u32[]{:S(2)}) copy-start(f32[640]{0:T(1024)} %param.9) | copy-start | bytes 7684
  36.9 77.5 %copy-start.4 = (s32[40]{0:T(128)S(1)}, s32[40]{0:T(128)}, u32[]{:S(2)}) copy-start(s32[40]{0:T(128)} %param.8) | copy-start | bytes 484
  42.4 83.2 %slice-start = ((s8[10485760]{0:T(1024)(128)(4,1)}), s8[2097152]{0:T(1024)(128)(4,1)S(1)}, s32[]{:S(2)}) async-start(s8[10485760]{0:T(1024)(128)(4,1)} %bitcast.70), calls=%async_computation.2 | async-start | bytes 4194304
  114.6 11.0 %slice-start.1 = ((s8[10485760]{0:T(1024)(128)(4,1)}), s8[4194304]{0:T(1024)(128)(4,1)S(1)}, s32[]{:S(2)}) async-start(s8[10485760]{0:T(1024)(128)(4,1)} %bitcast.70), calls=%async_computation.3 | async-start | bytes 8388608
  118.3 7.3 %slice-start.2 = ((s8[10485760]{0:T(1024)(128)(4,1)}), s8[4194304]{0:T(1024)(128)(4,1)S(1)}, s32[]{:S(2)}) async-start(s8[10485760]{0:T(1024)(128)(4,1)} %bitcast.70), calls=%async_computation.4 | async-start | bytes 8388608
  118.3 75.8 %copy-start.2 = (s32[16]{0:T(128)S(1)}, s32[16]{0:T(128)}, u32[]{:S(2)}) copy-start(s32[16]{0:T(128)} %param.7) | copy-start | bytes 196
Sparse Core Ops, SparseCore 0:
  128.4 65.5 reduce-scatter.1
where the time goes:
time: 207 us; the launch traced here: 205 us
  blocking collectives  93.1 us (45%)
  waiting for transfers between devices  65.8 us (32%)
  matrix products  29.5 us (14%)
  between operations  13.5 us (7%)
    psum x1, blocking collectives, per_device(): summed = lax.psum(data, 'param')  70.5 us
    reduce_scatter x1, waiting for transfers between devices, per_device(): lax.psum_scatter(adjoint, 'sensor', scatter_dimension=2, tiled=True)  65.7 us
    all_gather x1, blocking collectives, per_device(): piece = lax.all_gather(spectrum, 'sensor', axis=2, tiled=True)  22.6 us
  transfers between devices with their start and end apart: 1, of which 1 were waited for; matrix products, arithmetic and copies ran while one was open for 0% of the time, Pallas kernels for 0%

commit v1 on v0

v1 whole, which is shorter than its diff:
```python
import functools
import math

import jax
import jax.numpy as jnp
from jax import lax
from jax.experimental import pallas as pl
from jax.experimental.pallas import tpu as pltpu
from jax.sharding import PartitionSpec as P

F32 = jnp.float32
BF16 = jnp.bfloat16
VMEM = pl.BlockSpec(memory_space=pltpu.VMEM)
SIN_TERMS = (-1.0 / 6, 1.0 / 120, -1.0 / 5040, 1.0 / 362880, -1.0 / 39916800)
COS_TERMS = (-1.0 / 2, 1.0 / 24, -1.0 / 720, 1.0 / 40320, -1.0 / 3628800, 1.0 / 479001600)


def series(square, terms):
    total = jnp.full_like(square, terms[-1])
    for term in terms[-2::-1]:
        total = total * square + term
    return total


def trig_tables(frequency, step, num_steps):
    turns = (frequency * step).astype(F32)
    rest = turns - num_steps * jnp.floor(turns * (1.0 / num_steps))
    rest = jnp.where(rest < 0, rest + num_steps, rest)
    rest = jnp.where(rest >= num_steps, rest - num_steps, rest)
    rest = jnp.where(rest > num_steps / 2, rest - num_steps, rest)
    flip = jnp.abs(rest) > num_steps / 4
    near = jnp.where(flip, jnp.where(rest > 0, num_steps / 2, -num_steps / 2) - rest, rest)
    angle = near * (2.0 * math.pi / num_steps)
    square = angle * angle
    scale = 1.0 / math.sqrt(num_steps)
    cosine = (1.0 + square * series(square, COS_TERMS)) * jnp.where(flip, -scale, scale)
    sine = (angle + angle * square * series(square, SIN_TERMS)) * scale
    return cosine, sine


def split3(value):
    high = value.astype(BF16)
    rest = value - high.astype(F32)
    middle = rest.astype(BF16)
    low = (rest - middle.astype(F32)).astype(BF16)
    return high, middle, low


def dot(a, b, dims):
    return lax.dot_general(a, b, (dims, ((), ())), preferred_element_type=F32)


def table_of(frequencies_ref, num_freq, num_steps):
    frequency = frequencies_ref[...]
    step = lax.broadcasted_iota(jnp.int32, (num_freq, num_steps), 1)
    cosine, sine = trig_tables(frequency, step, num_steps)
    return jnp.concatenate([cosine, -sine], axis=0)


def spectrum_kernel(frequencies_ref, motion_ref, out_ref):
    num_freq = frequencies_ref.shape[0]
    num_steps = motion_ref.shape[0]
    rows = 2 * num_freq
    table = jnp.concatenate(split3(table_of(frequencies_ref, num_freq, num_steps)), axis=0)
    high, middle, low = split3(motion_ref[...])
    nn = ((1,), (0,))
    by_high = dot(table, high, nn)
    by_middle = dot(table[: 2 * rows], middle, nn)
    by_low = dot(table[:rows], low, nn)
    spectrum = (
        by_high[2 * rows :] + by_middle[rows:] + by_low + by_high[rows : 2 * rows] + by_middle[:rows]
    ) + by_high[:rows]
    out_ref[...] = jnp.broadcast_to(spectrum.astype(BF16)[None], out_ref.shape)


def swap_parts(row, sensors):
    lanes = row.shape[1]
    lane = lax.broadcasted_iota(jnp.int32, row.shape, 1)
    first = lax.rem(lane, 2 * sensors) < sensors
    return jnp.where(first, pltpu.roll(row, lanes - sensors, 1), pltpu.roll(row, sensors, 1)), first


def own_frequency(num_freq, lanes):
    freq = lax.broadcasted_iota(jnp.int32, (num_freq, lanes), 0)
    lane = lax.broadcasted_iota(jnp.int32, (num_freq, lanes), 1)
    each = lanes // num_freq
    return (lane >= freq * each) & (lane < (freq + 1) * each)


def forward_kernel(sensors, num_freq, spectrum_ref, blocks_ref, out_ref):
    pieces, _, width = spectrum_ref.shape
    lanes = blocks_ref.shape[0]
    total = jnp.zeros((2 * num_freq, lanes), F32)
    for piece in range(pieces):
        part = blocks_ref[:, piece * width : (piece + 1) * width]
        total += dot(spectrum_ref[piece], part, ((1,), (1,)))
    own = own_frequency(num_freq, lanes)
    by_real = jnp.sum(jnp.where(own, total[:num_freq], 0.0), axis=0, keepdims=True)
    by_imag = jnp.sum(jnp.where(own, total[num_freq:], 0.0), axis=0, keepdims=True)
    by_real = jnp.broadcast_to(by_real, (8, lanes))
    by_imag = jnp.broadcast_to(by_imag, (8, lanes))
    swapped, first = swap_parts(by_imag, sensors)
    data = by_real + jnp.where(first, -swapped, swapped)
    for piece in range(out_ref.shape[0]):
        out_ref[piece] = data[:1]


def backward_kernel(sensors, num_freq, data_ref, weight_ref, blocks_ref, out_ref):
    lanes = blocks_ref.shape[0]
    pieces, rows, width = out_ref.shape
    data = jnp.sum(data_ref[...], axis=0)
    weighted = jnp.broadcast_to(data * weight_ref[...], (8, lanes)).astype(BF16).astype(F32)
    swapped, first = swap_parts(weighted, sensors)
    turned = jnp.where(first, swapped, -swapped)
    own = own_frequency(num_freq, lanes)
    left = jnp.concatenate(
        [jnp.where(own, weighted[:1], 0.0), jnp.where(own, turned[:1], 0.0)], axis=0
    ).astype(BF16)
    for piece in range(pieces):
        part = blocks_ref[:, piece * width : (piece + 1) * width]
        out_ref[piece] = dot(left, part, ((1,), (0,))).astype(BF16)


def final_kernel(frequencies_ref, adjoint_ref, out_ref):
    num_freq = frequencies_ref.shape[0]
    num_steps = out_ref.shape[0]
    adjoint = jnp.sum(adjoint_ref[...].astype(F32), axis=0)
    th, tm, tl = split3(table_of(frequencies_ref, num_freq, num_steps))
    ah, am, al = split3(adjoint)
    left = jnp.concatenate([tl, tm, th, tm, th, th], axis=0)
    right = jnp.concatenate([ah, am, al, ah, am, ah], axis=0)
    out_ref[...] = dot(left, right, ((0,), (0,)))


def call(kernel, shape, dtype, args, limit):
    return pl.pallas_call(
        kernel,
        out_shape=jax.ShapeDtypeStruct(shape, dtype),
        in_specs=[VMEM] * len(args),
        out_specs=VMEM,
        compiler_params=pltpu.CompilerParams(vmem_limit_bytes=limit),
    )(*args)


def per_device(seafloor_motion, response_blocks, frequencies, station_of_row, noise_precision):
    num_freq, _, sensors, params = response_blocks.shape
    num_steps, width = seafloor_motion.shape
    rows = 2 * num_freq
    lanes = rows * sensors
    pieces = params // width
    blocks = response_blocks.reshape(lanes, params)
    column = frequencies[:, None]

    matches = station_of_row[:, None] == jnp.arange(noise_precision.shape[0], dtype=jnp.int32)[None, :]
    weight = jnp.sum(jnp.where(matches, noise_precision[None, :], 0.0), axis=1)
    weight = jnp.tile(weight, rows)[None]

    copies = call(
        spectrum_kernel, (pieces, rows, width), BF16, (column, seafloor_motion), 16 << 20
    )
    spectrum = lax.all_to_all(copies, "sensor", 0, 0)
    partial = call(
        functools.partial(forward_kernel, sensors, num_freq),
        (lax.axis_size("param"), 1, lanes),
        F32,
        (spectrum, blocks),
        16 << 20,
    )
    data = lax.all_to_all(partial, "param", 0, 0)
    pieces_out = call(
        functools.partial(backward_kernel, sensors, num_freq),
        (pieces, rows, width),
        BF16,
        (data, weight, blocks),
        16 << 20,
    )
    adjoint = lax.all_to_all(pieces_out, "sensor", 0, 0)
    return call(final_kernel, (num_steps, width), F32, (column, adjoint), 16 << 20)


def solution(mesh):
    in_specs = (
        P(None, ("param", "sensor")),
        P(None, None, "sensor", "param"),
        P(),
        P("sensor"),
        P(),
    )
    return jax.shard_map(
        per_device,
        mesh=mesh,
        in_specs=in_specs,
        out_specs=P(None, ("param", "sensor")),
        check_vma=False,
    )
```

time: 207 us -> 62.7 us (0.30)
  blocking collectives: 93.1 us -> 26.2 us
  waiting for transfers between devices: 65.8 us -> 8.7 us
  matrix products: 29.5 us -> 0 us
  between operations: 13.5 us -> 0.05 us
  starting transfers between devices: 0.01 us -> 10 us
  local copies, waits for them, and re-layouts: 1.06 us -> 9.87 us
  Pallas kernels: 0 us -> 7.29 us
    psum x1 -> x0, blocking collectives: 70.5 us -> none  [per_device(): summed = lax.psum(data, 'param')]
    reduce_scatter x1 -> x0, waiting for transfers between devices: 65.7 us -> none  [per_device(): lax.psum_scatter(adjoint, 'sensor', scatter_dimension=2, tiled=True)]
    dot_general x12 -> x0, matrix products: 29.5 us -> none  [the longest x1 3.99 us: per_device(): jnp.einsum('ksp,kp->ks', real_block, piece[:, 1], preferred_element_type=...]
    all_to_all x0 -> x2, blocking collectives: none -> 26.2 us  [the longest x1 14.1 us: per_device(): spectrum = lax.all_to_all(copies, 'sensor', 0, 0)]
    all_gather x1 -> x0, blocking collectives: 22.6 us -> none  [per_device(): piece = lax.all_gather(spectrum, 'sensor', axis=2, tiled=True)]
    all_to_all x0 -> x1, starting transfers between devices: none -> 10 us  [per_device(): data = lax.all_to_all(partial, 'param', 0, 0)]
    all_to_all x0 -> x1, waiting for transfers between devices: none -> 8.7 us  [per_device(): data = lax.all_to_all(partial, 'param', 0, 0)]
    unnamed x16 -> x10, local copies, waits for them, and re-layouts: 1.04 us -> 9.01 us
where the time goes in v1:
time: 62.7 us; the launch traced here: 62.3 us
  blocking collectives  26.2 us (42%)
  starting transfers between devices  10 us (16%)
  local copies, waits for them, and re-layouts  9.87 us (16%)
  waiting for transfers between devices  8.7 us (14%)
  Pallas kernels  7.29 us (12%)
    all_to_all x1, blocking collectives, per_device(): spectrum = lax.all_to_all(copies, 'sensor', 0, 0)  14.1 us
    all_to_all x1, blocking collectives, per_device(): adjoint = lax.all_to_all(pieces_out, 'sensor', 0, 0)  12 us
    all_to_all x1, starting transfers between devices, per_device(): data = lax.all_to_all(partial, 'param', 0, 0)  10 us
    unnamed x10, local copies, waits for them, and re-layouts  9.01 us
    all_to_all x1, waiting for transfers between devices, per_device(): data = lax.all_to_all(partial, 'param', 0, 0)  8.7 us
    pallas_call x4, Pallas kernels, call(): pl.pallas_call(kernel, out_shape=jax.ShapeDtypeStruct(shape, dtype), in_s...  7.29 us
  transfers between devices with their start and end apart: 1, of which 1 were waited for; matrix products, arithmetic and copies ran while one was open for 0% of the time, Pallas kernels for 0%

profile of v1, /device:TPU:1, one launch (start us, length us, event | category | flops | bytes accessed | tf_op | source)
XLA Modules:
  0.0 62.3 jit_solution(6412288256665136267)
XLA Ops:
  0.0 0.0 copy-start.3
  0.0 0.0 copy-start.4
  0.0 0.8 %copy.9.frequencies_ref = s32[16,1]{1,0:T(8,128)S(1)} copy(s32[16,1]{0,1:T(1,128)} %bitcast.4) | data formatting | bytes 128 | tf_op jit(solution)/shard_map/broadcast_in_dim | solution.py:152
  0.8 0.0 copy-start.2
  0.8 1.0 %copy-done.2 = f32[420,256]{1,0:T(8,128)S(1)} copy-done((f32[420,256]{1,0:T(8,128)S(1)}, f32[420,256]{1,0:T(8,128)}, u32[]{:S(2)}) %copy-start.2) | copy-done | bytes 430104
  1.8 0.3 shard_map.55
  2.1 14.1 %all_to_all.15.spectrum_ref = bf16[16,32,256]{2,1,0:T(8,128)(2,1)S(1)} all-to-all(bf16[16,32,256]{2,1,0:T(8,128)(2,1)S(1)} %shard_map.55), channel_id=1, replica_groups=mesh['param'=16,'sensor'=16] {'sensor'}, dimensions={0} | all-to-all | bytes 524288 | tf_op jit(solution)/shard_map/all_to_all | solution.py:161
  16.3 0.0 copy-start
  16.3 4.0 %copy-done = bf16[16,2,40,4096]{3,2,1,0:T(8,128)(2,1)S(1)} copy-done((bf16[16,2,40,4096]{3,2,1,0:T(8,128)(2,1)S(1)}, bf16[16,2,40,4096]{3,2,1,0:T(8,128)(2,1)}, u32[]{:S(2)}) %copy-start) | copy-done | bytes 10485784
  20.3 3.9 %shard_map.56 = f32[16,1,1280]{2,1,0:T(1,128)} custom-call(bf16[16,32,256]{2,1,0:T(8,128)(2,1)S(1)} %all_to_all.15.spectrum_ref, bf16[1280,4096]{1,0:T(8,128)(2,1)S(1)} %bitcast.2), custom_call_target="tpu_custom_call" | custom-call | tf_op jit(solution)/shard_map/pallas_call | solution.py:136
  24.1 10.0 %all-to-all-start.1 = ((f32[16,1,1280]{2,1,0:T(1,128)}), f32[16,1,1280]{2,1,0:T(1,128)S(1)}, u32[]{:S(2)}, u32[]{:S(2)}) async-start(f32[16,1,1280]{2,1,0:T(1,128)} %shard_map.56), calls=%async_computation.1 | async-start | bytes 163840 | tf_op jit(solution)/shard_map/all_to_all | solution.py:169
  34.2 0.0 copy-done.3
  34.2 0.0 copy-done.4
  34.2 0.2 select_reduce_fusion
  34.4 0.1 broadcast_in_dim_tile.3.weight_ref
  34.5 8.7 %all-to-all-done.1.data_ref = f32[16,1,1280]{2,1,0:T(1,128)S(1)} async-done(((f32[16,1,1280]{2,1,0:T(1,128)}), f32[16,1,1280]{2,1,0:T(1,128)S(1)}, u32[]{:S(2)}, u32[]{:S(2)}) %all-to-all-start.1) | async-done | bytes 81952 | tf_op jit(solution)/shard_map/all_to_all | solution.py:169
  43.2 0.0 copy-start.1
  43.2 4.0 %copy-done.1 = bf16[16,2,40,4096]{3,2,1,0:T(8,128)(2,1)S(1)} copy-done((bf16[16,2,40,4096]{3,2,1,0:T(8,128)(2,1)S(1)}, bf16[16,2,40,4096]{3,2,1,0:T(8,128)(2,1)}, u32[]{:S(2)}) %copy-start.1) | copy-done | bytes 10485784
  47.2 1.9 %shard_map.57 = bf16[16,32,256]{2,1,0:T(8,128)(2,1)S(1)} custom-call(f32[16,1,1280]{2,1,0:T(1,128)S(1)} %all-to-all-done.1.data_ref, f32[1,1280]{1,0:T(1,128)S(1)} %broadcast_in_dim_tile.3.weight_ref, bf16[1280,4096]{1,0:T(8,128)(2,1)S(1)} %bitcast.3), custom_call_target="tpu_custom_call" | custom-call | tf_op jit(solution)/shard_map/pallas_call | solution.py:136
  49.1 12.0 %all_to_all.16.adjoint_ref = bf16[16,32,256]{2,1,0:T(8,128)(2,1)S(1)} all-to-all(bf16[16,32,256]{2,1,0:T(8,128)(2,1)S(1)} %shard_map.57), channel_id=1, replica_groups=mesh['param'=16,'sensor'=16] {'sensor'}, dimensions={0} | all-to-all | bytes 524288 | tf_op jit(solution)/shard_map/all_to_all | solution.py:177
  61.2 1.1 %shard_map.58 = f32[420,256]{1,0:T(8,128)} custom-call(s32[16,1]{1,0:T(8,128)S(1)} %copy.9.frequencies_ref, bf16[16,32,256]{2,1,0:T(8,128)(2,1)S(1)} %all_to_all.16.adjoint_ref), custom_call_target="tpu_custom_call" | custom-call | tf_op jit(solution)/shard_map/pallas_call | solution.py:136
  (1 shorter events, 0.0 us)
Async XLA Ops:
  0.0 34.2 %copy-start.3 = (f32[640]{0:T(1024)S(1)}, f32[640]{0:T(1024)}, u32[]{:S(2)}) copy-start(f32[640]{0:T(1024)} %param.9) | copy-start | bytes 7684
  0.0 34.2 %copy-start.4 = (s32[40]{0:T(128)S(1)}, s32[40]{0:T(128)}, u32[]{:S(2)}) copy-start(s32[40]{0:T(128)} %param.8) | copy-start | bytes 484
  0.8 1.0 %copy-start.2 = (f32[420,256]{1,0:T(8,128)S(1)}, f32[420,256]{1,0:T(8,128)}, u32[]{:S(2)}) copy-start(f32[420,256]{1,0:T(8,128)} %motion_ref.1) | copy-start | bytes 1290244
  16.3 4.0 %copy-start = (bf16[16,2,40,4096]{3,2,1,0:T(8,128)(2,1)S(1)}, bf16[16,2,40,4096]{3,2,1,0:T(8,128)(2,1)}, u32[]{:S(2)}) copy-start(bf16[16,2,40,4096]{3,2,1,0:T(8,128)(2,1)} %param.6) | copy-start | bytes 31457284
  24.1 19.0 %all-to-all-start.1 = ((f32[16,1,1280]{2,1,0:T(1,128)}), f32[16,1,1280]{2,1,0:T(1,128)S(1)}, u32[]{:S(2)}, u32[]{:S(2)}) async-start(f32[16,1,1280]{2,1,0:T(1,128)} %shard_map.56), calls=%async_computation.1 | async-start | bytes 163840 | tf_op jit(solution)/shard_map/all_to_all | solution.py:169
  43.2 4.0 %copy-start.1 = (bf16[16,2,40,4096]{3,2,1,0:T(8,128)(2,1)S(1)}, bf16[16,2,40,4096]{3,2,1,0:T(8,128)(2,1)}, u32[]{:S(2)}) copy-start(bf16[16,2,40,4096]{3,2,1,0:T(8,128)(2,1)} %param.6) | copy-start | bytes 31457284

commit v2 on v1

--- a/solution.py
+++ b/solution.py
@@ -11,6 +11,7 @@
 F32 = jnp.float32
 BF16 = jnp.bfloat16
 VMEM = pl.BlockSpec(memory_space=pltpu.VMEM)
+HBM = pl.BlockSpec(memory_space=pltpu.HBM)
 SIN_TERMS = (-1.0 / 6, 1.0 / 120, -1.0 / 5040, 1.0 / 362880, -1.0 / 39916800)
 COS_TERMS = (-1.0 / 2, 1.0 / 24, -1.0 / 720, 1.0 / 40320, -1.0 / 3628800, 1.0 / 479001600)
 
@@ -50,18 +51,56 @@
     return lax.dot_general(a, b, (dims, ((), ())), preferred_element_type=F32)
 
 
-def table_of(frequencies_ref, num_freq, num_steps):
-    frequency = frequencies_ref[...]
+def column_of(row):
+    size = row.shape[1]
+    across = lax.broadcasted_iota(jnp.int32, (size, size), 1)
+    down = lax.broadcasted_iota(jnp.int32, (size, size), 0)
+    return jnp.sum(jnp.where(across == down, row, jnp.zeros_like(row)), axis=1, keepdims=True)
+
+
+def spectrum_kernel(
+    frequencies_hbm, motion_hbm, station_hbm, noise_hbm, out_ref, table_ref, weight_ref,
+    frequencies_ref, motion_ref, station_ref, noise_ref, sems,
+):
+    copies = [
+        pltpu.make_async_copy(source, target, sems.at[i])
+        for i, (source, target) in enumerate(
+            [
+                (frequencies_hbm, frequencies_ref),
+                (station_hbm, station_ref),
+                (noise_hbm, noise_ref),
+                (motion_hbm, motion_ref),
+            ]
+        )
+    ]
+    for copy in copies:
+        copy.start()
+    num_freq = frequencies_ref.shape[1]
+    num_steps = motion_ref.shape[0]
+    rows = 2 * num_freq
+
+    copies[0].wait()
+    frequency = column_of(frequencies_ref[...])
     step = lax.broadcasted_iota(jnp.int32, (num_freq, num_steps), 1)
     cosine, sine = trig_tables(frequency, step, num_steps)
-    return jnp.concatenate([cosine, -sine], axis=0)
-
-
-def spectrum_kernel(frequencies_ref, motion_ref, out_ref):
-    num_freq = frequencies_ref.shape[0]
-    num_steps = motion_ref.shape[0]
-    rows = 2 * num_freq
-    table = jnp.concatenate(split3(table_of(frequencies_ref, num_freq, num_steps)), axis=0)
+    table = jnp.concatenate(split3(jnp.concatenate([cosine, -sine], axis=0)), axis=0)
+    table_ref[...] = table
+
+    copies[1].wait()
+    copies[2].wait()
+    sensors, lanes = station_ref.shape[1], weight_ref.shape[1]
+    station = column_of(station_ref[...])
+    runs, length = noise_ref.shape
+    place = lax.broadcasted_iota(jnp.int32, (sensors, length), 1)
+    found = jnp.zeros((sensors, length), F32)
+    for run in range(runs):
+        found += jnp.where(station == place + run * length, noise_ref[run : run + 1], 0.0)
+    by_sensor = jnp.sum(found, axis=1, keepdims=True)
+    sensor = lax.broadcasted_iota(jnp.int32, (sensors, lanes), 0)
+    lane = lax.rem(lax.broadcasted_iota(jnp.int32, (1, lanes), 1), sensors)
+    weight_ref[...] = jnp.sum(jnp.where(sensor == lane, by_sensor, 0.0), axis=0, keepdims=True)
+
+    copies[3].wait()
     high, middle, low = split3(motion_ref[...])
     nn = ((1,), (0,))
     by_high = dot(table, high, nn)
@@ -88,12 +127,10 @@
 
 
 def forward_kernel(sensors, num_freq, spectrum_ref, blocks_ref, out_ref):
-    pieces, _, width = spectrum_ref.shape
+    pieces = spectrum_ref.shape[0]
     lanes = blocks_ref.shape[0]
-    total = jnp.zeros((2 * num_freq, lanes), F32)
-    for piece in range(pieces):
-        part = blocks_ref[:, piece * width : (piece + 1) * width]
-        total += dot(spectrum_ref[piece], part, ((1,), (1,)))
+    spectrum = jnp.concatenate([spectrum_ref[piece] for piece in range(pieces)], axis=1)
+    total = dot(blocks_ref[...], spectrum, ((1,), (1,))).T
     own = own_frequency(num_freq, lanes)
     by_real = jnp.sum(jnp.where(own, total[:num_freq], 0.0), axis=0, keepdims=True)
     by_imag = jnp.sum(jnp.where(own, total[num_freq:], 0.0), axis=0, keepdims=True)
@@ -121,24 +158,27 @@
         out_ref[piece] = dot(left, part, ((1,), (0,))).astype(BF16)
 
 
-def final_kernel(frequencies_ref, adjoint_ref, out_ref):
-    num_freq = frequencies_ref.shape[0]
-    num_steps = out_ref.shape[0]
+def final_kernel(table_ref, adjoint_ref, out_ref):
+    rows = adjoint_ref.shape[1]
     adjoint = jnp.sum(adjoint_ref[...].astype(F32), axis=0)
-    th, tm, tl = split3(table_of(frequencies_ref, num_freq, num_steps))
+    table = table_ref[...]
+    th, tm, tl = table[:rows], table[rows : 2 * rows], table[2 * rows :]
     ah, am, al = split3(adjoint)
     left = jnp.concatenate([tl, tm, th, tm, th, th], axis=0)
     right = jnp.concatenate([ah, am, al, ah, am, ah], axis=0)
     out_ref[...] = dot(left, right, ((0,), (0,)))
 
 
-def call(kernel, shape, dtype, args, limit):
+def call(kernel, outs, args, spaces=None, scratch=(), cost=None):
+    spaces = spaces or [VMEM] * len(args)
     return pl.pallas_call(
         kernel,
-        out_shape=jax.ShapeDtypeStruct(shape, dtype),
-        in_specs=[VMEM] * len(args),
-        out_specs=VMEM,
-        compiler_params=pltpu.CompilerParams(vmem_limit_bytes=limit),
+        out_shape=[jax.ShapeDtypeStruct(shape, dtype) for shape, dtype in outs],
+        in_specs=spaces,
+        out_specs=[VMEM] * len(outs),
+        scratch_shapes=scratch,
+        compiler_params=pltpu.CompilerParams(vmem_limit_bytes=16 << 20),
+        cost_estimate=cost,
     )(*args)
 
 
@@ -149,33 +189,33 @@
     lanes = rows * sensors
     pieces = params // width
     blocks = response_blocks.reshape(lanes, params)
-    column = frequencies[:, None]
-
-    matches = station_of_row[:, None] == jnp.arange(noise_precision.shape[0], dtype=jnp.int32)[None, :]
-    weight = jnp.sum(jnp.where(matches, noise_precision[None, :], 0.0), axis=1)
-    weight = jnp.tile(weight, rows)[None]
-
-    copies = call(
-        spectrum_kernel, (pieces, rows, width), BF16, (column, seafloor_motion), 16 << 20
+    small = (frequencies[None], seafloor_motion, station_of_row[None], noise_precision.reshape(-1, 128))
+    small = tuple(pltpu.with_memory_space_constraint(x, pltpu.HBM) for x in small)
+    busy = pl.CostEstimate(flops=20 * 10**9, bytes_accessed=64 << 20, transcendentals=0)
+
+    copies, table, weight = call(
+        spectrum_kernel,
+        [((pieces, rows, width), BF16), ((3 * rows, num_steps), BF16), ((1, lanes), F32)],
+        small,
+        [HBM] * len(small),
+        [pltpu.VMEM(x.shape, x.dtype) for x in small] + [pltpu.SemaphoreType.DMA((len(small),))],
+        busy,
     )
     spectrum = lax.all_to_all(copies, "sensor", 0, 0)
-    partial = call(
+    (partial,) = call(
         functools.partial(forward_kernel, sensors, num_freq),
-        (lax.axis_size("param"), 1, lanes),
-        F32,
+        [((lax.axis_size("param"), 1, lanes), F32)],
         (spectrum, blocks),
-        16 << 20,
+        cost=busy,
     )
     data = lax.all_to_all(partial, "param", 0, 0)
-    pieces_out = call(
+    (pieces_out,) = call(
         functools.partial(backward_kernel, sensors, num_freq),
-        (pieces, rows, width),
-        BF16,
+        [((pieces, rows, width), BF16)],
         (data, weight, blocks),
-        16 << 20,
     )
     adjoint = lax.all_to_all(pieces_out, "sensor", 0, 0)
-    return call(final_kernel, (num_steps, width), F32, (column, adjoint), 16 << 20)
+    return call(final_kernel, [((num_steps, width), F32)], (table, adjoint))[0]
 
 
 def solution(mesh):

time: 62.7 us -> 53 us (0.85)
  blocking collectives: 26.2 us -> 45.3 us
  starting transfers between devices: 10 us -> 0 us
  local copies, waits for them, and re-layouts: 9.87 us -> 0.01 us
  waiting for transfers between devices: 8.7 us -> 0 us
    all_to_all x0 -> x1, blocking collectives: none -> 18.8 us  [per_device(): data = lax.all_to_all(partial, 'param', 0, 0)]
    all_to_all x1 -> x0, starting transfers between devices: 10 us -> none  [per_device(): data = lax.all_to_all(partial, 'param', 0, 0)]
    unnamed x10 -> x2, local copies, waits for them, and re-layouts: 9.01 us -> 0.01 us
    all_to_all x1 -> x0, waiting for transfers between devices: 8.7 us -> none  [per_device(): data = lax.all_to_all(partial, 'param', 0, 0)]
    broadcast_in_dim x1 -> x0, local copies, waits for them, and re-layouts: 0.76 us -> none  [per_device(): column = frequencies[:, None]]
  transfers between devices with their start and end apart: 1 -> 0, of which waited for: 1 -> 0; matrix products, arithmetic and copies ran while one was open for 0% -> 0% of each run, Pallas kernels for 0% -> 0%
where the time goes in v2:
time: 53 us; the launch traced here: 52.8 us
  blocking collectives  45.3 us (85%)
  Pallas kernels  7.48 us (14%)
    all_to_all x1, blocking collectives, per_device(): data = lax.all_to_all(partial, 'param', 0, 0)  18.8 us
    all_to_all x1, blocking collectives, per_device(): spectrum = lax.all_to_all(copies, 'sensor', 0, 0)  14.4 us
    all_to_all x1, blocking collectives, per_device(): adjoint = lax.all_to_all(pieces_out, 'sensor', 0, 0)  12 us
    pallas_call x4, Pallas kernels, call(): pl.pallas_call(kernel, out_shape=[jax.ShapeDtypeStruct(shape, dtype) for...  7.48 us

profile of v2, /device:TPU:1, one launch (start us, length us, event | category | flops | bytes accessed | tf_op | source)
XLA Modules:
  0.0 52.8 jit_solution(17049304808327995599)
XLA Ops:
  0.0 0.0 copy-start
  0.0 1.5 %shard_map.55 = (bf16[16,32,256]{2,1,0:T(8,128)(2,1)S(1)}, bf16[96,420]{1,0:T(8,128)(2,1)S(1)}, f32[1,1280]{1,0:T(1,128)S(1)}) custom-call(s32[1,16]{1,0:T(1,128)} %bitcast.7, f32[420,256]{1,0:T(8,128)} %motion_hbm.1, s32[1,40]{1,0:T(1,128)} %bitcast.8, f32[5,128]{1,0:T(8,128)} %bitcast.6), custom_call_target="tpu_custom_call" | custom-call | flops 20000000000 | bytes 67108864 | tf_op jit(solution)/shard_map/pallas_call | solution.py:174
  1.5 14.4 %all_to_all.15.spectrum_ref = bf16[16,32,256]{2,1,0:T(8,128)(2,1)S(1)} all-to-all(bf16[16,32,256]{2,1,0:T(8,128)(2,1)S(1)} %get-tuple-element.9), channel_id=1, replica_groups=mesh['param'=16,'sensor'=16] {'sensor'}, dimensions={0} | all-to-all | bytes 524288 | tf_op jit(solution)/shard_map/all_to_all | solution.py:204
  15.9 0.0 copy-done
  15.9 3.0 %shard_map.56 = f32[16,1,1280]{2,1,0:T(1,128)S(1)} custom-call(bf16[16,32,256]{2,1,0:T(8,128)(2,1)S(1)} %all_to_all.15.spectrum_ref, bf16[1280,4096]{1,0:T(8,128)(2,1)S(1)} %bitcast.4), custom_call_target="tpu_custom_call" | custom-call | flops 20000000000 | bytes 67108864 | tf_op jit(solution)/shard_map/pallas_call | solution.py:174
  18.9 18.8 %all_to_all.16.data_ref = f32[16,1,1280]{2,1,0:T(1,128)S(1)} all-to-all(f32[16,1,1280]{2,1,0:T(1,128)S(1)} %shard_map.56), channel_id=1, replica_groups=mesh['param'=16,'sensor'=16] {'param'}, dimensions={0} | all-to-all | bytes 163840 | tf_op jit(solution)/shard_map/all_to_all | solution.py:211
  37.8 1.9 %shard_map.57 = bf16[16,32,256]{2,1,0:T(8,128)(2,1)S(1)} custom-call(f32[16,1,1280]{2,1,0:T(1,128)S(1)} %all_to_all.16.data_ref, f32[1,1280]{1,0:T(1,128)S(1)} %get-tuple-element.10.weight_ref, bf16[1280,4096]{1,0:T(8,128)(2,1)S(1)} %bitcast.5), custom_call_target="tpu_custom_call" | custom-call | tf_op jit(solution)/shard_map/pallas_call | solution.py:174
  39.7 12.0 %all_to_all.17.adjoint_ref = bf16[16,32,256]{2,1,0:T(8,128)(2,1)S(1)} all-to-all(bf16[16,32,256]{2,1,0:T(8,128)(2,1)S(1)} %shard_map.57), channel_id=1, replica_groups=mesh['param'=16,'sensor'=16] {'sensor'}, dimensions={0} | all-to-all | bytes 524288 | tf_op jit(solution)/shard_map/all_to_all | solution.py:217
  51.8 1.0 %shard_map.58 = f32[420,256]{1,0:T(8,128)} custom-call(bf16[96,420]{1,0:T(8,128)(2,1)S(1)} %get-tuple-element.8.table_ref, bf16[16,32,256]{2,1,0:T(8,128)(2,1)S(1)} %all_to_all.17.adjoint_ref), custom_call_target="tpu_custom_call" | custom-call | tf_op jit(solution)/shard_map/pallas_call | solution.py:174
Async XLA Ops:
  0.0 15.9 %copy-start = (bf16[16,2,40,4096]{3,2,1,0:T(8,128)(2,1)S(1)}, bf16[16,2,40,4096]{3,2,1,0:T(8,128)(2,1)}, u32[]{:S(2)}) copy-start(bf16[16,2,40,4096]{3,2,1,0:T(8,128)(2,1)} %param.6) | copy-start | bytes 31457284

commit v3 on v2

--- a/solution.py
+++ b/solution.py
@@ -126,11 +126,28 @@
     return (lane >= freq * each) & (lane < (freq + 1) * each)
 
 
-def forward_kernel(sensors, num_freq, spectrum_ref, blocks_ref, out_ref):
-    pieces = spectrum_ref.shape[0]
+def own_core():
+    return lax.rem(lax.axis_index("sensor"), 2)
+
+
+def piece_columns(piece, core, width):
+    return pl.ds(pl.multiple_of((2 * piece + core) * width, width), width)
+
+
+def half_forward(spectrum_ref, blocks_ref, core):
+    pieces, _, width = spectrum_ref.shape
+    spectrum = jnp.concatenate([spectrum_ref[piece] for piece in range(pieces)], axis=1)
+    columns = [blocks_ref[:, piece_columns(piece, core, width)] for piece in range(pieces)]
+    return dot(jnp.concatenate(columns, axis=1), spectrum, ((1,), (1,)))
+
+
+def own_forward_kernel(spectrum_ref, blocks_ref, out_ref):
+    out_ref[...] = half_forward(spectrum_ref, blocks_ref, own_core())
+
+
+def other_forward_kernel(sensors, num_freq, spectrum_ref, own_ref, blocks_ref, out_ref):
     lanes = blocks_ref.shape[0]
-    spectrum = jnp.concatenate([spectrum_ref[piece] for piece in range(pieces)], axis=1)
-    total = dot(blocks_ref[...], spectrum, ((1,), (1,))).T
+    total = (own_ref[...] + half_forward(spectrum_ref, blocks_ref, 1 - own_core())).T
     own = own_frequency(num_freq, lanes)
     by_real = jnp.sum(jnp.where(own, total[:num_freq], 0.0), axis=0, keepdims=True)
     by_imag = jnp.sum(jnp.where(own, total[num_freq:], 0.0), axis=0, keepdims=True)
@@ -142,9 +159,9 @@
         out_ref[piece] = data[:1]
 
 
-def backward_kernel(sensors, num_freq, data_ref, weight_ref, blocks_ref, out_ref):
+def other_backward_kernel(sensors, num_freq, data_ref, weight_ref, blocks_ref, out_ref, left_ref):
     lanes = blocks_ref.shape[0]
-    pieces, rows, width = out_ref.shape
+    pieces, _, width = out_ref.shape
     data = jnp.sum(data_ref[...], axis=0)
     weighted = jnp.broadcast_to(data * weight_ref[...], (8, lanes)).astype(BF16).astype(F32)
     swapped, first = swap_parts(weighted, sensors)
@@ -153,9 +170,29 @@
     left = jnp.concatenate(
         [jnp.where(own, weighted[:1], 0.0), jnp.where(own, turned[:1], 0.0)], axis=0
     ).astype(BF16)
+    left_ref[...] = left
+    other = 1 - own_core()
     for piece in range(pieces):
-        part = blocks_ref[:, piece * width : (piece + 1) * width]
+        part = blocks_ref[:, piece_columns(piece, other, width)]
         out_ref[piece] = dot(left, part, ((1,), (0,))).astype(BF16)
+
+
+def own_backward_kernel(left_ref, blocks_ref, out_ref):
+    pieces, _, width = out_ref.shape
+    for piece in range(pieces):
+        part = blocks_ref[:, piece_columns(piece, own_core(), width)]
+        out_ref[piece] = dot(left_ref[...], part, ((1,), (0,)))
+
+
+def joined_backward_kernel(left_ref, blocks_ref, first_ref, arrived_ref, out_ref):
+    done, _, width = first_ref.shape
+    pieces = out_ref.shape[0]
+    for piece in range(done, pieces):
+        part = blocks_ref[:, piece_columns(piece, own_core(), width)]
+        product = dot(left_ref[...], part, ((1,), (0,)))
+        out_ref[piece] = (product + arrived_ref[piece].astype(F32)).astype(BF16)
+    for piece in range(done):
+        out_ref[piece] = (first_ref[piece] + arrived_ref[piece].astype(F32)).astype(BF16)
 
 
 def final_kernel(table_ref, adjoint_ref, out_ref):
@@ -192,29 +229,41 @@
     small = (frequencies[None], seafloor_motion, station_of_row[None], noise_precision.reshape(-1, 128))
     small = tuple(pltpu.with_memory_space_constraint(x, pltpu.HBM) for x in small)
     busy = pl.CostEstimate(flops=20 * 10**9, bytes_accessed=64 << 20, transcendentals=0)
+    half = pieces // 2
+    cores = [[2 * piece + core for piece in range(half)] for core in range(2)]
+    swap = [(device, device ^ 1) for device in range(pieces)]
+    ahead = (half * 5) // 8
 
     copies, table, weight = call(
         spectrum_kernel,
-        [((pieces, rows, width), BF16), ((3 * rows, num_steps), BF16), ((1, lanes), F32)],
+        [((half, rows, width), BF16), ((3 * rows, num_steps), BF16), ((1, lanes), F32)],
         small,
         [HBM] * len(small),
         [pltpu.VMEM(x.shape, x.dtype) for x in small] + [pltpu.SemaphoreType.DMA((len(small),))],
         busy,
     )
-    spectrum = lax.all_to_all(copies, "sensor", 0, 0)
+    spectrum = lax.all_to_all(copies, "sensor", 0, 0, axis_index_groups=cores)
+    other_spectrum = lax.ppermute(spectrum, "sensor", swap)
+    (own,) = call(own_forward_kernel, [((lanes, rows), F32)], (spectrum, blocks), cost=busy)
     (partial,) = call(
-        functools.partial(forward_kernel, sensors, num_freq),
+        functools.partial(other_forward_kernel, sensors, num_freq),
         [((lax.axis_size("param"), 1, lanes), F32)],
-        (spectrum, blocks),
+        (other_spectrum, own, blocks),
         cost=busy,
     )
     data = lax.all_to_all(partial, "param", 0, 0)
-    (pieces_out,) = call(
-        functools.partial(backward_kernel, sensors, num_freq),
-        [((pieces, rows, width), BF16)],
+    to_other, left = call(
+        functools.partial(other_backward_kernel, sensors, num_freq),
+        [((half, rows, width), BF16), ((rows, lanes), BF16)],
         (data, weight, blocks),
-    )
-    adjoint = lax.all_to_all(pieces_out, "sensor", 0, 0)
+        cost=busy,
+    )
+    arrived = lax.ppermute(to_other, "sensor", swap)
+    (first,) = call(own_backward_kernel, [((ahead, rows, width), F32)], (left, blocks), cost=busy)
+    (joined,) = call(
+        joined_backward_kernel, [((half, rows, width), BF16)], (left, blocks, first, arrived), cost=busy
+    )
+    adjoint = lax.all_to_all(joined, "sensor", 0, 0, axis_index_groups=cores)
     return call(final_kernel, [((num_steps, width), F32)], (table, adjoint))[0]
 
 

time: 53 us -> 50.7 us (0.957)
  blocking collectives: 45.3 us -> 38.7 us
  starting transfers between devices: 0 us -> 3.64 us
    all_to_all x2, blocking collectives: 26.4 us -> 19.9 us  [the longest x1 11.8 us: per_device(): spectrum = lax.all_to_all(copies, 'sensor', 0, 0, axis_index_groups=cores)]
    ppermute x0 -> x2, starting transfers between devices: none -> 3.64 us  [the longest x1 2.08 us: per_device(): other_spectrum = lax.ppermute(spectrum, 'sensor', swap)]
    pallas_call x4 -> x7, Pallas kernels: 7.48 us -> 7.88 us  [call(): pl.pallas_call(kernel, out_shape=[jax.ShapeDtypeStruct(shape, dtype) for...]
  transfers between devices with their start and end apart: 0 -> 2, of which waited for: 0 -> 1; matrix products, arithmetic and copies ran while one was open for 0% -> 0% of each run, Pallas kernels for 0% -> 4%
where the time goes in v3:
time: 50.7 us; the launch traced here: 50.6 us
  blocking collectives  38.7 us (76%)
  Pallas kernels  7.88 us (16%)
  starting transfers between devices  3.64 us (7%)
    all_to_all x1, blocking collectives, per_device(): data = lax.all_to_all(partial, 'param', 0, 0)  18.8 us
    all_to_all x1, blocking collectives, per_device(): spectrum = lax.all_to_all(copies, 'sensor', 0, 0, axis_index_groups=cores)  11.8 us
    all_to_all x1, blocking collectives, per_device(): adjoint = lax.all_to_all(joined, 'sensor', 0, 0, axis_index_groups=cores)  8.03 us
    pallas_call x7, Pallas kernels, call(): pl.pallas_call(kernel, out_shape=[jax.ShapeDtypeStruct(shape, dtype) for...  7.88 us
    ppermute x1, starting transfers between devices, per_device(): other_spectrum = lax.ppermute(spectrum, 'sensor', swap)  2.08 us
    ppermute x1, starting transfers between devices, per_device(): arrived = lax.ppermute(to_other, 'sensor', swap)  1.57 us
  transfers between devices with their start and end apart: 2, of which 1 were waited for; matrix products, arithmetic and copies ran while one was open for 0% of the time, Pallas kernels for 4%

profile of v3, /device:TPU:1, one launch (start us, length us, event | category | flops | bytes accessed | tf_op | source)
XLA Modules:
  0.0 50.6 jit_solution(4754645442626289931)
XLA Ops:
  0.0 0.0 copy-start
  0.0 1.5 %shard_map.55 = (bf16[8,32,256]{2,1,0:T(8,128)(2,1)S(1)}, bf16[96,420]{1,0:T(8,128)(2,1)S(1)}, f32[1,1280]{1,0:T(1,128)S(1)}) custom-call(s32[1,16]{1,0:T(1,128)} %bitcast.10, f32[420,256]{1,0:T(8,128)} %motion_hbm.1, s32[1,40]{1,0:T(1,128)} %bitcast.11, f32[5,128]{1,0:T(8,128)} %bitcast.9), custom_call_target="tpu_custom_call" | custom-call | flops 20000000000 | bytes 67108864 | tf_op jit(solution)/shard_map/pallas_call | solution.py:211
  1.5 11.8 %all_to_all.15.spectrum_ref = bf16[8,32,256]{2,1,0:T(8,128)(2,1)S(1)} all-to-all(bf16[8,32,256]{2,1,0:T(8,128)(2,1)S(1)} %get-tuple-element.11), channel_id=1, replica_groups={{0,2,4,6,8,10,12,14},{1,3,5,7,9,11,13,15},{16,18,20,22,24,26,28,30},{17..., dimensions={0} | all-to-all | bytes 262144 | tf_op jit(solution)/shard_map/all_to_all | solution.py:245
  13.3 2.1 %collective-permute-start = (bf16[8,32,256]{2,1,0:T(8,128)(2,1)S(1)}, bf16[8,32,256]{2,1,0:T(8,128)(2,1)S(1)}, u32[]{:S(2)}, u32[]{:S(2)}) collective-permute-start(bf16[8,32,256]{2,1,0:T(8,128)(2,1)S(1)} %all_to_all.15.spectrum_ref), channel_id=1, source_target_pairs={{0,1},{1,0},{2,3},{3,2},{4,5},{5,4},{6,7},{7,6},{8,9},{9,8},{10,11... | collective-permute-start | bytes 393224 | tf_op jit(solution)/shard_map/ppermute | solution.py:246
  15.4 0.0 copy-done
  15.4 1.5 %shard_map.56.own_ref = f32[1280,32]{1,0:T(8,128)S(1)} custom-call(bf16[8,32,256]{2,1,0:T(8,128)(2,1)S(1)} %all_to_all.15.spectrum_ref, bf16[1280,4096]{1,0:T(8,128)(2,1)S(1)} %bitcast.4), custom_call_target="tpu_custom_call" | custom-call | flops 20000000000 | bytes 67108864 | tf_op jit(solution)/shard_map/pallas_call | solution.py:211
  16.9 0.0 collective-permute-done.spectrum_ref
  16.9 1.7 %shard_map.57 = f32[16,1,1280]{2,1,0:T(1,128)S(1)} custom-call(bf16[8,32,256]{2,1,0:T(8,128)(2,1)S(1)} %collective-permute-done.spectrum_ref, f32[1280,32]{1,0:T(8,128)S(1)} %shard_map.56.own_ref, bf16[1280,4096]{1,0:T(8,128)(2,1)S(1)} %bitcast.5), custom_call_target="tpu_custom_call" | custom-call | flops 20000000000 | bytes 67108864 | tf_op jit(solution)/shard_map/pallas_call | solution.py:211
  18.6 18.8 %all_to_all.16.data_ref = f32[16,1,1280]{2,1,0:T(1,128)S(1)} all-to-all(f32[16,1,1280]{2,1,0:T(1,128)S(1)} %shard_map.57), channel_id=1, replica_groups=mesh['param'=16,'sensor'=16] {'param'}, dimensions={0} | all-to-all | bytes 163840 | tf_op jit(solution)/shard_map/all_to_all | solution.py:254
  37.4 1.0 %shard_map.58 = (bf16[8,32,256]{2,1,0:T(8,128)(2,1)S(1)}, bf16[32,1280]{1,0:T(8,128)(2,1)S(1)}) custom-call(f32[16,1,1280]{2,1,0:T(1,128)S(1)} %all_to_all.16.data_ref, f32[1,1280]{1,0:T(1,128)S(1)} %get-tuple-element.12.weight_ref, bf16[1280,4096]{1,0:T(8,128)(2,1)S(1)} %bitcast.6), custom_call_target="tpu_custom_call" | custom-call | flops 20000000000 | bytes 67108864 | tf_op jit(solution)/shard_map/pallas_call | solution.py:211
  38.5 1.6 %collective-permute-start.1 = (bf16[8,32,256]{2,1,0:T(8,128)(2,1)S(1)}, bf16[8,32,256]{2,1,0:T(8,128)(2,1)S(1)}, u32[]{:S(2)}, u32[]{:S(2)}) collective-permute-start(bf16[8,32,256]{2,1,0:T(8,128)(2,1)S(1)} %get-tuple-element.14), channel_id=1, source_target_pairs={{0,1},{1,0},{2,3},{3,2},{4,5},{5,4},{6,7},{7,6},{8,9},{9,8},{10,11... | collective-permute-start | bytes 393224 | tf_op jit(solution)/shard_map/ppermute | solution.py:261
  40.0 0.7 %shard_map.59.first_ref = f32[5,32,256]{2,1,0:T(8,128)S(1)} custom-call(bf16[32,1280]{1,0:T(8,128)(2,1)S(1)} %get-tuple-element.13.left_ref, bf16[1280,4096]{1,0:T(8,128)(2,1)S(1)} %bitcast.7), custom_call_target="tpu_custom_call" | custom-call | flops 20000000000 | bytes 67108864 | tf_op jit(solution)/shard_map/pallas_call | solution.py:211
  40.7 0.3 collective-permute-done.1.arrived_ref
  41.0 0.5 shard_map.60
  41.5 8.0 %all_to_all.17.adjoint_ref = bf16[8,32,256]{2,1,0:T(8,128)(2,1)S(1)} all-to-all(bf16[8,32,256]{2,1,0:T(8,128)(2,1)S(1)} %shard_map.60), channel_id=1, replica_groups={{0,2,4,6,8,10,12,14},{1,3,5,7,9,11,13,15},{16,18,20,22,24,26,28,30},{17..., dimensions={0} | all-to-all | bytes 262144 | tf_op jit(solution)/shard_map/all_to_all | solution.py:266
  49.5 1.0 %shard_map.61 = f32[420,256]{1,0:T(8,128)} custom-call(bf16[96,420]{1,0:T(8,128)(2,1)S(1)} %get-tuple-element.10.table_ref, bf16[8,32,256]{2,1,0:T(8,128)(2,1)S(1)} %all_to_all.17.adjoint_ref), custom_call_target="tpu_custom_call" | custom-call | tf_op jit(solution)/shard_map/pallas_call | solution.py:211
Async XLA Ops:
  0.0 15.4 %copy-start = (bf16[16,2,40,4096]{3,2,1,0:T(8,128)(2,1)S(1)}, bf16[16,2,40,4096]{3,2,1,0:T(8,128)(2,1)}, u32[]{:S(2)}) copy-start(bf16[16,2,40,4096]{3,2,1,0:T(8,128)(2,1)} %param.6) | copy-start | bytes 31457284
  13.3 3.6 %collective-permute-start = (bf16[8,32,256]{2,1,0:T(8,128)(2,1)S(1)}, bf16[8,32,256]{2,1,0:T(8,128)(2,1)S(1)}, u32[]{:S(2)}, u32[]{:S(2)}) collective-permute-start(bf16[8,32,256]{2,1,0:T(8,128)(2,1)S(1)} %all_to_all.15.spectrum_ref), channel_id=1, source_target_pairs={{0,1},{1,0},{2,3},{3,2},{4,5},{5,4},{6,7},{7,6},{8,9},{9,8},{10,11... | collective-permute-start | bytes 393224 | tf_op jit(solution)/shard_map/ppermute | solution.py:246
  38.5 2.6 %collective-permute-start.1 = (bf16[8,32,256]{2,1,0:T(8,128)(2,1)S(1)}, bf16[8,32,256]{2,1,0:T(8,128)(2,1)S(1)}, u32[]{:S(2)}, u32[]{:S(2)}) collective-permute-start(bf16[8,32,256]{2,1,0:T(8,128)(2,1)S(1)} %get-tuple-element.14), channel_id=1, source_target_pairs={{0,1},{1,0},{2,3},{3,2},{4,5},{5,4},{6,7},{7,6},{8,9},{9,8},{10,11... | collective-permute-start | bytes 393224 | tf_op jit(solution)/shard_map/ppermute | solution.py:261

commit v4 on v3

--- a/solution.py
+++ b/solution.py
@@ -184,15 +184,8 @@
         out_ref[piece] = dot(left_ref[...], part, ((1,), (0,)))
 
 
-def joined_backward_kernel(left_ref, blocks_ref, first_ref, arrived_ref, out_ref):
-    done, _, width = first_ref.shape
-    pieces = out_ref.shape[0]
-    for piece in range(done, pieces):
-        part = blocks_ref[:, piece_columns(piece, own_core(), width)]
-        product = dot(left_ref[...], part, ((1,), (0,)))
-        out_ref[piece] = (product + arrived_ref[piece].astype(F32)).astype(BF16)
-    for piece in range(done):
-        out_ref[piece] = (first_ref[piece] + arrived_ref[piece].astype(F32)).astype(BF16)
+def joined_kernel(first_ref, arrived_ref, out_ref):
+    out_ref[...] = (first_ref[...] + arrived_ref[...].astype(F32)).astype(BF16)
 
 
 def final_kernel(table_ref, adjoint_ref, out_ref):
@@ -232,7 +225,6 @@
     half = pieces // 2
     cores = [[2 * piece + core for piece in range(half)] for core in range(2)]
     swap = [(device, device ^ 1) for device in range(pieces)]
-    ahead = (half * 5) // 8
 
     copies, table, weight = call(
         spectrum_kernel,
@@ -259,10 +251,8 @@
         cost=busy,
     )
     arrived = lax.ppermute(to_other, "sensor", swap)
-    (first,) = call(own_backward_kernel, [((ahead, rows, width), F32)], (left, blocks), cost=busy)
-    (joined,) = call(
-        joined_backward_kernel, [((half, rows, width), BF16)], (left, blocks, first, arrived), cost=busy
-    )
+    (first,) = call(own_backward_kernel, [((half, rows, width), F32)], (left, blocks), cost=busy)
+    (joined,) = call(joined_kernel, [((half, rows, width), BF16)], (first, arrived), cost=busy)
     adjoint = lax.all_to_all(joined, "sensor", 0, 0, axis_index_groups=cores)
     return call(final_kernel, [((num_steps, width), F32)], (table, adjoint))[0]
 

time: 50.7 us -> 50.3 us (level)
  transfers between devices with their start and end apart: 2 -> 2, of which waited for: 1 -> 0; matrix products, arithmetic and copies ran while one was open for 0% -> 0% of each run, Pallas kernels for 4% -> 5%
where the time goes in v4:
time: 50.3 us; the launch traced here: 50.1 us
  blocking collectives  38.6 us (77%)
  Pallas kernels  7.77 us (15%)
  starting transfers between devices  3.64 us (7%)
    all_to_all x1, blocking collectives, per_device(): data = lax.all_to_all(partial, 'param', 0, 0)  18.8 us
    all_to_all x1, blocking collectives, per_device(): spectrum = lax.all_to_all(copies, 'sensor', 0, 0, axis_index_groups=cores)  11.8 us
    all_to_all x1, blocking collectives, per_device(): adjoint = lax.all_to_all(joined, 'sensor', 0, 0, axis_index_groups=cores)  7.97 us
    pallas_call x7, Pallas kernels, call(): pl.pallas_call(kernel, out_shape=[jax.ShapeDtypeStruct(shape, dtype) for...  7.77 us
    ppermute x1, starting transfers between devices, per_device(): other_spectrum = lax.ppermute(spectrum, 'sensor', swap)  2.08 us
    ppermute x1, starting transfers between devices, per_device(): arrived = lax.ppermute(to_other, 'sensor', swap)  1.57 us
  transfers between devices with their start and end apart: 2, of which 0 were waited for; matrix products, arithmetic and copies ran while one was open for 0% of the time, Pallas kernels for 5%

profile of v4, /device:TPU:1, one launch (start us, length us, event | category | flops | bytes accessed | tf_op | source)
XLA Modules:
  0.0 50.1 jit_solution(14071146713066294699)
XLA Ops:
  0.0 0.0 copy-start
  0.0 1.5 %shard_map.55 = (bf16[8,32,256]{2,1,0:T(8,128)(2,1)S(1)}, bf16[96,420]{1,0:T(8,128)(2,1)S(1)}, f32[1,1280]{1,0:T(1,128)S(1)}) custom-call(s32[1,16]{1,0:T(1,128)} %bitcast.9, f32[420,256]{1,0:T(8,128)} %motion_hbm.1, s32[1,40]{1,0:T(1,128)} %bitcast.10, f32[5,128]{1,0:T(8,128)} %bitcast.8), custom_call_target="tpu_custom_call" | custom-call | flops 20000000000 | bytes 67108864 | tf_op jit(solution)/shard_map/pallas_call | solution.py:204
  1.5 11.8 %all_to_all.15.spectrum_ref = bf16[8,32,256]{2,1,0:T(8,128)(2,1)S(1)} all-to-all(bf16[8,32,256]{2,1,0:T(8,128)(2,1)S(1)} %get-tuple-element.11), channel_id=1, replica_groups={{0,2,4,6,8,10,12,14},{1,3,5,7,9,11,13,15},{16,18,20,22,24,26,28,30},{17..., dimensions={0} | all-to-all | bytes 262144 | tf_op jit(solution)/shard_map/all_to_all | solution.py:237
  13.3 2.1 %collective-permute-start = (bf16[8,32,256]{2,1,0:T(8,128)(2,1)S(1)}, bf16[8,32,256]{2,1,0:T(8,128)(2,1)S(1)}, u32[]{:S(2)}, u32[]{:S(2)}) collective-permute-start(bf16[8,32,256]{2,1,0:T(8,128)(2,1)S(1)} %all_to_all.15.spectrum_ref), channel_id=1, source_target_pairs={{0,1},{1,0},{2,3},{3,2},{4,5},{5,4},{6,7},{7,6},{8,9},{9,8},{10,11... | collective-permute-start | bytes 393224 | tf_op jit(solution)/shard_map/ppermute | solution.py:238
  15.4 0.0 copy-done
  15.4 1.5 %shard_map.56.own_ref = f32[1280,32]{1,0:T(8,128)S(1)} custom-call(bf16[8,32,256]{2,1,0:T(8,128)(2,1)S(1)} %all_to_all.15.spectrum_ref, bf16[1280,4096]{1,0:T(8,128)(2,1)S(1)} %bitcast.4), custom_call_target="tpu_custom_call" | custom-call | flops 20000000000 | bytes 67108864 | tf_op jit(solution)/shard_map/pallas_call | solution.py:204
  16.9 0.0 collective-permute-done.spectrum_ref
  16.9 1.7 %shard_map.57 = f32[16,1,1280]{2,1,0:T(1,128)S(1)} custom-call(bf16[8,32,256]{2,1,0:T(8,128)(2,1)S(1)} %collective-permute-done.spectrum_ref, f32[1280,32]{1,0:T(8,128)S(1)} %shard_map.56.own_ref, bf16[1280,4096]{1,0:T(8,128)(2,1)S(1)} %bitcast.5), custom_call_target="tpu_custom_call" | custom-call | flops 20000000000 | bytes 67108864 | tf_op jit(solution)/shard_map/pallas_call | solution.py:204
  18.6 18.8 %all_to_all.16.data_ref = f32[16,1,1280]{2,1,0:T(1,128)S(1)} all-to-all(f32[16,1,1280]{2,1,0:T(1,128)S(1)} %shard_map.57), channel_id=1, replica_groups=mesh['param'=16,'sensor'=16] {'param'}, dimensions={0} | all-to-all | bytes 163840 | tf_op jit(solution)/shard_map/all_to_all | solution.py:246
  37.4 1.0 %shard_map.58 = (bf16[8,32,256]{2,1,0:T(8,128)(2,1)S(1)}, bf16[32,1280]{1,0:T(8,128)(2,1)S(1)}) custom-call(f32[16,1,1280]{2,1,0:T(1,128)S(1)} %all_to_all.16.data_ref, f32[1,1280]{1,0:T(1,128)S(1)} %get-tuple-element.12.weight_ref, bf16[1280,4096]{1,0:T(8,128)(2,1)S(1)} %bitcast.6), custom_call_target="tpu_custom_call" | custom-call | flops 20000000000 | bytes 67108864 | tf_op jit(solution)/shard_map/pallas_call | solution.py:204
  38.5 1.6 %collective-permute-start.1 = (bf16[8,32,256]{2,1,0:T(8,128)(2,1)S(1)}, bf16[8,32,256]{2,1,0:T(8,128)(2,1)S(1)}, u32[]{:S(2)}, u32[]{:S(2)}) collective-permute-start(bf16[8,32,256]{2,1,0:T(8,128)(2,1)S(1)} %get-tuple-element.14), channel_id=1, source_target_pairs={{0,1},{1,0},{2,3},{3,2},{4,5},{5,4},{6,7},{7,6},{8,9},{9,8},{10,11... | collective-permute-start | bytes 393224 | tf_op jit(solution)/shard_map/ppermute | solution.py:253
  40.0 1.0 %shard_map.59.first_ref = f32[8,32,256]{2,1,0:T(8,128)S(1)} custom-call(bf16[32,1280]{1,0:T(8,128)(2,1)S(1)} %get-tuple-element.13.left_ref, bf16[1280,4096]{1,0:T(8,128)(2,1)S(1)} %bitcast.7), custom_call_target="tpu_custom_call" | custom-call | flops 20000000000 | bytes 67108864 | tf_op jit(solution)/shard_map/pallas_call | solution.py:204
  41.1 0.0 collective-permute-done.1.arrived_ref
  41.1 8.0 %all_to_all.17.adjoint_ref = bf16[8,32,256]{2,1,0:T(8,128)(2,1)S(1)} all-to-all(bf16[8,32,256]{2,1,0:T(8,128)(2,1)S(1)} %shard_map.60), channel_id=1, replica_groups={{0,2,4,6,8,10,12,14},{1,3,5,7,9,11,13,15},{16,18,20,22,24,26,28,30},{17..., dimensions={0} | all-to-all | bytes 262144 | tf_op jit(solution)/shard_map/all_to_all | solution.py:256
  49.1 1.0 %shard_map.61 = f32[420,256]{1,0:T(8,128)} custom-call(bf16[96,420]{1,0:T(8,128)(2,1)S(1)} %get-tuple-element.10.table_ref, bf16[8,32,256]{2,1,0:T(8,128)(2,1)S(1)} %all_to_all.17.adjoint_ref), custom_call_target="tpu_custom_call" | custom-call | tf_op jit(solution)/shard_map/pallas_call | solution.py:204
  (1 shorter events, 0.0 us)
Async XLA Ops:
  0.0 15.4 %copy-start = (bf16[16,2,40,4096]{3,2,1,0:T(8,128)(2,1)S(1)}, bf16[16,2,40,4096]{3,2,1,0:T(8,128)(2,1)}, u32[]{:S(2)}) copy-start(bf16[16,2,40,4096]{3,2,1,0:T(8,128)(2,1)} %param.6) | copy-start | bytes 31457284
  13.3 3.6 %collective-permute-start = (bf16[8,32,256]{2,1,0:T(8,128)(2,1)S(1)}, bf16[8,32,256]{2,1,0:T(8,128)(2,1)S(1)}, u32[]{:S(2)}, u32[]{:S(2)}) collective-permute-start(bf16[8,32,256]{2,1,0:T(8,128)(2,1)S(1)} %all_to_all.15.spectrum_ref), channel_id=1, source_target_pairs={{0,1},{1,0},{2,3},{3,2},{4,5},{5,4},{6,7},{7,6},{8,9},{9,8},{10,11... | collective-permute-start | bytes 393224 | tf_op jit(solution)/shard_map/ppermute | solution.py:238
  38.5 2.6 %collective-permute-start.1 = (bf16[8,32,256]{2,1,0:T(8,128)(2,1)S(1)}, bf16[8,32,256]{2,1,0:T(8,128)(2,1)S(1)}, u32[]{:S(2)}, u32[]{:S(2)}) collective-permute-start(bf16[8,32,256]{2,1,0:T(8,128)(2,1)S(1)} %get-tuple-element.14), channel_id=1, source_target_pairs={{0,1},{1,0},{2,3},{3,2},{4,5},{5,4},{6,7},{7,6},{8,9},{9,8},{10,11... | collective-permute-start | bytes 393224 | tf_op jit(solution)/shard_map/ppermute | solution.py:253

commit v5 on v4

--- a/solution.py
+++ b/solution.py
@@ -9,6 +9,8 @@
 from jax.sharding import PartitionSpec as P
 
 F32 = jnp.float32
+STAGES = ((1,), (3,), (4,), (12,))
+PLACES = (0, 5, 2, 7, 4, 1, 6, 3)
 BF16 = jnp.bfloat16
 VMEM = pl.BlockSpec(memory_space=pltpu.VMEM)
 HBM = pl.BlockSpec(memory_space=pltpu.HBM)
@@ -131,7 +133,7 @@
 
 
 def piece_columns(piece, core, width):
-    return pl.ds(pl.multiple_of((2 * piece + core) * width, width), width)
+    return pl.ds(pl.multiple_of((2 * PLACES[piece] + core) * width, width), width)
 
 
 def half_forward(spectrum_ref, blocks_ref, core):
@@ -155,14 +157,24 @@
     by_imag = jnp.broadcast_to(by_imag, (8, lanes))
     swapped, first = swap_parts(by_imag, sensors)
     data = by_real + jnp.where(first, -swapped, swapped)
-    for piece in range(out_ref.shape[0]):
-        out_ref[piece] = data[:1]
-
-
-def other_backward_kernel(sensors, num_freq, data_ref, weight_ref, blocks_ref, out_ref, left_ref):
+    out_ref[...] = data[:1]
+
+
+def sum_kernel(own_ref, *refs):
+    *arrived, out_ref = refs
+    total = own_ref[...]
+    for ref in arrived:
+        total += ref[...]
+    out_ref[...] = total
+
+
+def other_backward_kernel(sensors, num_freq, weight_ref, blocks_ref, *refs):
+    *data_refs, out_ref, left_ref = refs
     lanes = blocks_ref.shape[0]
     pieces, _, width = out_ref.shape
-    data = jnp.sum(data_ref[...], axis=0)
+    data = data_refs[0][...]
+    for ref in data_refs[1:]:
+        data += ref[...]
     weighted = jnp.broadcast_to(data * weight_ref[...], (8, lanes)).astype(BF16).astype(F32)
     swapped, first = swap_parts(weighted, sensors)
     turned = jnp.where(first, swapped, -swapped)
@@ -223,7 +235,7 @@
     small = tuple(pltpu.with_memory_space_constraint(x, pltpu.HBM) for x in small)
     busy = pl.CostEstimate(flops=20 * 10**9, bytes_accessed=64 << 20, transcendentals=0)
     half = pieces // 2
-    cores = [[2 * piece + core for piece in range(half)] for core in range(2)]
+    cores = [[2 * place + core for place in PLACES] for core in range(2)]
     swap = [(device, device ^ 1) for device in range(pieces)]
 
     copies, table, weight = call(
@@ -239,15 +251,23 @@
     (own,) = call(own_forward_kernel, [((lanes, rows), F32)], (spectrum, blocks), cost=busy)
     (partial,) = call(
         functools.partial(other_forward_kernel, sensors, num_freq),
-        [((lax.axis_size("param"), 1, lanes), F32)],
+        [((1, lanes), F32)],
         (other_spectrum, own, blocks),
         cost=busy,
     )
-    data = lax.all_to_all(partial, "param", 0, 0)
+    row = [((1, lanes), F32)]
+
+    def partners(value, bits):
+        count = lax.axis_size("param")
+        return [lax.ppermute(value, "param", [(i, i ^ bit) for i in range(count)]) for bit in bits]
+
+    some = partial
+    for bits in STAGES[:-1]:
+        (some,) = call(sum_kernel, row, (some, *partners(some, bits)))
     to_other, left = call(
         functools.partial(other_backward_kernel, sensors, num_freq),
         [((half, rows, width), BF16), ((rows, lanes), BF16)],
-        (data, weight, blocks),
+        (weight, blocks, some, *partners(some, STAGES[-1])),
         cost=busy,
     )
     arrived = lax.ppermute(to_other, "sensor", swap)

time: 50.3 us -> 49.7 us (0.988)
  blocking collectives: 38.6 us -> 19.4 us
  starting transfers between devices: 3.64 us -> 18 us
  waiting for transfers between devices: 0.01 us -> 4.19 us
    all_to_all x1 -> x0, blocking collectives: 18.8 us -> none  [per_device(): data = lax.all_to_all(partial, 'param', 0, 0)]
    ppermute x0 -> x4, starting transfers between devices: none -> 11.6 us  [partners(): lax.ppermute(value, 'param', [(i, i ^ bit) for i in range(count)])]
    ppermute x0 -> x4, waiting for transfers between devices: none -> 4.19 us  [partners(): lax.ppermute(value, 'param', [(i, i ^ bit) for i in range(count)])]
    ppermute x1, starting transfers between devices: 1.57 us -> 4.28 us  [per_device(): arrived = lax.ppermute(to_other, 'sensor', swap)]
    pallas_call x7 -> x10, Pallas kernels: 7.77 us -> 7.74 us  [call(): pl.pallas_call(kernel, out_shape=[jax.ShapeDtypeStruct(shape, dtype) for...]
  transfers between devices with their start and end apart: 2 -> 6, of which waited for: 0 -> 4; matrix products, arithmetic and copies ran while one was open for 0% -> 0% of each run, Pallas kernels for 5% -> 5%
where the time goes in v5:
time: 49.7 us; the launch traced here: 49.3 us
  blocking collectives  19.4 us (39%)
  starting transfers between devices  18 us (36%)
  Pallas kernels  7.74 us (16%)
  waiting for transfers between devices  4.19 us (8%)
    all_to_all x1, blocking collectives, per_device(): spectrum = lax.all_to_all(copies, 'sensor', 0, 0, axis_index_groups=cores)  11.6 us
    ppermute x4, starting transfers between devices, partners(): lax.ppermute(value, 'param', [(i, i ^ bit) for i in range(count)])  11.6 us
    all_to_all x1, blocking collectives, per_device(): adjoint = lax.all_to_all(joined, 'sensor', 0, 0, axis_index_groups=cores)  7.75 us
    pallas_call x10, Pallas kernels, call(): pl.pallas_call(kernel, out_shape=[jax.ShapeDtypeStruct(shape, dtype) for...  7.74 us
    ppermute x1, starting transfers between devices, per_device(): arrived = lax.ppermute(to_other, 'sensor', swap)  4.28 us
    ppermute x4, waiting for transfers between devices, partners(): lax.ppermute(value, 'param', [(i, i ^ bit) for i in range(count)])  4.19 us
    ppermute x1, starting transfers between devices, per_device(): other_spectrum = lax.ppermute(spectrum, 'sensor', swap)  2.09 us
  transfers between devices with their start and end apart: 6, of which 4 were waited for; matrix products, arithmetic and copies ran while one was open for 0% of the time, Pallas kernels for 5%

profile of v5, /device:TPU:1, one launch (start us, length us, event | category | flops | bytes accessed | tf_op | source)
XLA Modules:
  0.0 49.3 jit_solution(2520085850909695371)
XLA Ops:
  0.0 0.0 copy-start
  0.0 1.5 %shard_map.55 = (bf16[8,32,256]{2,1,0:T(8,128)(2,1)S(1)}, bf16[96,420]{1,0:T(8,128)(2,1)S(1)}, f32[1,1280]{1,0:T(1,128)S(1)}) custom-call(s32[1,16]{1,0:T(1,128)} %bitcast.9, f32[420,256]{1,0:T(8,128)} %motion_hbm.1, s32[1,40]{1,0:T(1,128)} %bitcast.10, f32[5,128]{1,0:T(8,128)} %bitcast.8), custom_call_target="tpu_custom_call" | custom-call | flops 20000000000 | bytes 67108864 | tf_op jit(solution)/shard_map/pallas_call | solution.py:216
  1.5 11.6 %all_to_all.10.spectrum_ref = bf16[8,32,256]{2,1,0:T(8,128)(2,1)S(1)} all-to-all(bf16[8,32,256]{2,1,0:T(8,128)(2,1)S(1)} %get-tuple-element.12), channel_id=1, replica_groups={{0,10,4,14,8,2,12,6},{1,11,5,15,9,3,13,7},{16,26,20,30,24,18,28,22},{17..., dimensions={0} | all-to-all | bytes 262144 | tf_op jit(solution)/shard_map/all_to_all | solution.py:249
  13.1 2.1 %collective-permute-start = (bf16[8,32,256]{2,1,0:T(8,128)(2,1)S(1)}, bf16[8,32,256]{2,1,0:T(8,128)(2,1)S(1)}, u32[]{:S(2)}, u32[]{:S(2)}) collective-permute-start(bf16[8,32,256]{2,1,0:T(8,128)(2,1)S(1)} %all_to_all.10.spectrum_ref), channel_id=1, source_target_pairs={{0,1},{1,0},{2,3},{3,2},{4,5},{5,4},{6,7},{7,6},{8,9},{9,8},{10,11... | collective-permute-start | bytes 393224 | tf_op jit(solution)/shard_map/ppermute | solution.py:250
  15.2 0.0 copy-done
  15.2 1.5 %shard_map.56.own_ref = f32[1280,32]{1,0:T(8,128)S(1)} custom-call(bf16[8,32,256]{2,1,0:T(8,128)(2,1)S(1)} %all_to_all.10.spectrum_ref, bf16[1280,4096]{1,0:T(8,128)(2,1)S(1)} %bitcast.4), custom_call_target="tpu_custom_call" | custom-call | flops 20000000000 | bytes 67108864 | tf_op jit(solution)/shard_map/pallas_call | solution.py:216
  16.7 0.0 collective-permute-done.spectrum_ref
  16.8 1.6 %shard_map.57.own_ref = f32[1,1280]{1,0:T(1,128)S(1)} custom-call(bf16[8,32,256]{2,1,0:T(8,128)(2,1)S(1)} %collective-permute-done.spectrum_ref, f32[1280,32]{1,0:T(8,128)S(1)} %shard_map.56.own_ref, bf16[1280,4096]{1,0:T(8,128)(2,1)S(1)} %bitcast.5), custom_call_target="tpu_custom_call" | custom-call | flops 20000000000 | bytes 67108864 | tf_op jit(solution)/shard_map/pallas_call | solution.py:216
  18.4 1.4 %collective-permute-start.1 = (f32[1,1280]{1,0:T(1,128)S(1)}, f32[1,1280]{1,0:T(1,128)S(1)}, u32[]{:S(2)}, u32[]{:S(2)}) collective-permute-start(f32[1,1280]{1,0:T(1,128)S(1)} %shard_map.57.own_ref), channel_id=1, source_target_pairs={{0,16},{16,0},{32,48},{48,32},{64,80},{80,64},{96,112},{112,96},{1... | collective-permute-start | bytes 15368 | tf_op jit(solution)/shard_map/ppermute | solution.py:262
  19.8 1.2 %collective-permute-done.1.refs_0_ = f32[1,1280]{1,0:T(1,128)S(1)} collective-permute-done((f32[1,1280]{1,0:T(1,128)S(1)}, f32[1,1280]{1,0:T(1,128)S(1)}, u32[]{:S(2)}, u32[]{:S(2)}) %collective-permute-start.1) | collective-permute-done | bytes 5152 | tf_op jit(solution)/shard_map/ppermute | solution.py:262
  21.0 2.7 %collective-permute-start.2 = (f32[1,1280]{1,0:T(1,128)S(1)}, f32[1,1280]{1,0:T(1,128)S(1)}, u32[]{:S(2)}, u32[]{:S(2)}) collective-permute-start(f32[1,1280]{1,0:T(1,128)S(1)} %shard_map.58.own_ref), channel_id=1, source_target_pairs={{0,48},{16,32},{32,16},{48,0},{64,112},{80,96},{96,80},{112,64},{1... | collective-permute-start | bytes 15368 | tf_op jit(solution)/shard_map/ppermute | solution.py:262
  23.7 1.0 %collective-permute-done.2.refs_0_ = f32[1,1280]{1,0:T(1,128)S(1)} collective-permute-done((f32[1,1280]{1,0:T(1,128)S(1)}, f32[1,1280]{1,0:T(1,128)S(1)}, u32[]{:S(2)}, u32[]{:S(2)}) %collective-permute-start.2) | collective-permute-done | bytes 5152 | tf_op jit(solution)/shard_map/ppermute | solution.py:262
  24.7 3.0 %collective-permute-start.3 = (f32[1,1280]{1,0:T(1,128)S(1)}, f32[1,1280]{1,0:T(1,128)S(1)}, u32[]{:S(2)}, u32[]{:S(2)}) collective-permute-start(f32[1,1280]{1,0:T(1,128)S(1)} %shard_map.59.own_ref), channel_id=1, source_target_pairs={{0,64},{16,80},{32,96},{48,112},{64,0},{80,16},{96,32},{112,48},{1... | collective-permute-start | bytes 15368 | tf_op jit(solution)/shard_map/ppermute | solution.py:262
  27.7 1.0 %collective-permute-done.3.refs_0_ = f32[1,1280]{1,0:T(1,128)S(1)} collective-permute-done((f32[1,1280]{1,0:T(1,128)S(1)}, f32[1,1280]{1,0:T(1,128)S(1)}, u32[]{:S(2)}, u32[]{:S(2)}) %collective-permute-start.3) | collective-permute-done | bytes 5152 | tf_op jit(solution)/shard_map/ppermute | solution.py:262
  28.7 4.5 %collective-permute-start.4 = (f32[1,1280]{1,0:T(1,128)S(1)}, f32[1,1280]{1,0:T(1,128)S(1)}, u32[]{:S(2)}, u32[]{:S(2)}) collective-permute-start(f32[1,1280]{1,0:T(1,128)S(1)} %shard_map.60.refs_0_), channel_id=1, source_target_pairs={{0,192},{16,208},{32,224},{48,240},{64,128},{80,144},{96,160},{112... | collective-permute-start | bytes 15368 | tf_op jit(solution)/shard_map/ppermute | solution.py:262
  33.2 1.0 %collective-permute-done.4.refs_1_ = f32[1,1280]{1,0:T(1,128)S(1)} collective-permute-done((f32[1,1280]{1,0:T(1,128)S(1)}, f32[1,1280]{1,0:T(1,128)S(1)}, u32[]{:S(2)}, u32[]{:S(2)}) %collective-permute-start.4) | collective-permute-done | bytes 5152 | tf_op jit(solution)/shard_map/ppermute | solution.py:262
  34.2 1.0 %shard_map.61 = (bf16[8,32,256]{2,1,0:T(8,128)(2,1)S(1)}, bf16[32,1280]{1,0:T(8,128)(2,1)S(1)}) custom-call(f32[1,1280]{1,0:T(1,128)S(1)} %get-tuple-element.11.weight_ref, bf16[1280,4096]{1,0:T(8,128)(2,1)S(1)} %bitcast.6, f32[1,1280]{1,0:T(1,128)S(1)} %shard_map.60.refs_0_, f32[1,1280]{1,0:T(1,128)S(1)} %collective-permute-done.4.refs_1_), custom_call_target="tpu_custom_call" | custom-call | flops 20000000000 | bytes 67108864 | tf_op jit(solution)/shard_map/pallas_call | solution.py:216
  35.2 4.3 %collective-permute-start.5 = (bf16[8,32,256]{2,1,0:T(8,128)(2,1)S(1)}, bf16[8,32,256]{2,1,0:T(8,128)(2,1)S(1)}, u32[]{:S(2)}, u32[]{:S(2)}) collective-permute-start(bf16[8,32,256]{2,1,0:T(8,128)(2,1)S(1)} %get-tuple-element.14), channel_id=1, source_target_pairs={{0,1},{1,0},{2,3},{3,2},{4,5},{5,4},{6,7},{7,6},{8,9},{9,8},{10,11... | collective-permute-start | bytes 393224 | tf_op jit(solution)/shard_map/ppermute | solution.py:273
  39.5 1.0 %shard_map.62.first_ref = f32[8,32,256]{2,1,0:T(8,128)S(1)} custom-call(bf16[32,1280]{1,0:T(8,128)(2,1)S(1)} %get-tuple-element.13.left_ref, bf16[1280,4096]{1,0:T(8,128)(2,1)S(1)} %bitcast.7), custom_call_target="tpu_custom_call" | custom-call | flops 20000000000 | bytes 67108864 | tf_op jit(solution)/shard_map/pallas_call | solution.py:216
  40.5 0.0 collective-permute-done.5.arrived_ref
  40.6 7.7 %all_to_all.11.adjoint_ref = bf16[8,32,256]{2,1,0:T(8,128)(2,1)S(1)} all-to-all(bf16[8,32,256]{2,1,0:T(8,128)(2,1)S(1)} %shard_map.63), channel_id=1, replica_groups={{0,10,4,14,8,2,12,6},{1,11,5,15,9,3,13,7},{16,26,20,30,24,18,28,22},{17..., dimensions={0} | all-to-all | bytes 262144 | tf_op jit(solution)/shard_map/all_to_all | solution.py:276
  48.3 1.0 %shard_map.64 = f32[420,256]{1,0:T(8,128)} custom-call(bf16[96,420]{1,0:T(8,128)(2,1)S(1)} %get-tuple-element.10.table_ref, bf16[8,32,256]{2,1,0:T(8,128)(2,1)S(1)} %all_to_all.11.adjoint_ref), custom_call_target="tpu_custom_call" | custom-call | tf_op jit(solution)/shard_map/pallas_call | solution.py:216
  (4 shorter events, 0.0 us)
Async XLA Ops:
  0.0 15.2 %copy-start = (bf16[16,2,40,4096]{3,2,1,0:T(8,128)(2,1)S(1)}, bf16[16,2,40,4096]{3,2,1,0:T(8,128)(2,1)}, u32[]{:S(2)}) copy-start(bf16[16,2,40,4096]{3,2,1,0:T(8,128)(2,1)} %param.6) | copy-start | bytes 31457284
  13.1 3.6 %collective-permute-start = (bf16[8,32,256]{2,1,0:T(8,128)(2,1)S(1)}, bf16[8,32,256]{2,1,0:T(8,128)(2,1)S(1)}, u32[]{:S(2)}, u32[]{:S(2)}) collective-permute-start(bf16[8,32,256]{2,1,0:T(8,128)(2,1)S(1)} %all_to_all.10.spectrum_ref), channel_id=1, source_target_pairs={{0,1},{1,0},{2,3},{3,2},{4,5},{5,4},{6,7},{7,6},{8,9},{9,8},{10,11... | collective-permute-start | bytes 393224 | tf_op jit(solution)/shard_map/ppermute | solution.py:250
  18.4 2.6 %collective-permute-start.1 = (f32[1,1280]{1,0:T(1,128)S(1)}, f32[1,1280]{1,0:T(1,128)S(1)}, u32[]{:S(2)}, u32[]{:S(2)}) collective-permute-start(f32[1,1280]{1,0:T(1,128)S(1)} %shard_map.57.own_ref), channel_id=1, source_target_pairs={{0,16},{16,0},{32,48},{48,32},{64,80},{80,64},{96,112},{112,96},{1... | collective-permute-start | bytes 15368 | tf_op jit(solution)/shard_map/ppermute | solution.py:262
  21.0 3.7 %collective-permute-start.2 = (f32[1,1280]{1,0:T(1,128)S(1)}, f32[1,1280]{1,0:T(1,128)S(1)}, u32[]{:S(2)}, u32[]{:S(2)}) collective-permute-start(f32[1,1280]{1,0:T(1,128)S(1)} %shard_map.58.own_ref), channel_id=1, source_target_pairs={{0,48},{16,32},{32,16},{48,0},{64,112},{80,96},{96,80},{112,64},{1... | collective-permute-start | bytes 15368 | tf_op jit(solution)/shard_map/ppermute | solution.py:262
  24.7 4.0 %collective-permute-start.3 = (f32[1,1280]{1,0:T(1,128)S(1)}, f32[1,1280]{1,0:T(1,128)S(1)}, u32[]{:S(2)}, u32[]{:S(2)}) collective-permute-start(f32[1,1280]{1,0:T(1,128)S(1)} %shard_map.59.own_ref), channel_id=1, source_target_pairs={{0,64},{16,80},{32,96},{48,112},{64,0},{80,16},{96,32},{112,48},{1... | collective-permute-start | bytes 15368 | tf_op jit(solution)/shard_map/ppermute | solution.py:262
  28.7 5.5 %collective-permute-start.4 = (f32[1,1280]{1,0:T(1,128)S(1)}, f32[1,1280]{1,0:T(1,128)S(1)}, u32[]{:S(2)}, u32[]{:S(2)}) collective-permute-start(f32[1,1280]{1,0:T(1,128)S(1)} %shard_map.60.refs_0_), channel_id=1, source_target_pairs={{0,192},{16,208},{32,224},{48,240},{64,128},{80,144},{96,160},{112... | collective-permute-start | bytes 15368 | tf_op jit(solution)/shard_map/ppermute | solution.py:262
  35.2 5.3 %collective-permute-start.5 = (bf16[8,32,256]{2,1,0:T(8,128)(2,1)S(1)}, bf16[8,32,256]{2,1,0:T(8,128)(2,1)S(1)}, u32[]{:S(2)}, u32[]{:S(2)}) collective-permute-start(bf16[8,32,256]{2,1,0:T(8,128)(2,1)S(1)} %get-tuple-element.14), channel_id=1, source_target_pairs={{0,1},{1,0},{2,3},{3,2},{4,5},{5,4},{6,7},{7,6},{8,9},{9,8},{10,11... | collective-permute-start | bytes 393224 | tf_op jit(solution)/shard_map/ppermute | solution.py:273

commit v6 on v5

--- a/solution.py
+++ b/solution.py
@@ -132,6 +132,17 @@
     return lax.rem(lax.axis_index("sensor"), 2)
 
 
+def own_mix():
+    device = lax.axis_index("sensor")
+    return lax.rem(device + lax.div(device, 2), 2)
+
+
+def mixed_columns(piece, mix, width):
+    place = PLACES[piece]
+    device = 2 * place + (1 - mix if place % 2 else mix)
+    return pl.ds(pl.multiple_of(device * width, width), width)
+
+
 def piece_columns(piece, core, width):
     return pl.ds(pl.multiple_of((2 * PLACES[piece] + core) * width, width), width)
 
@@ -139,17 +150,17 @@
 def half_forward(spectrum_ref, blocks_ref, core):
     pieces, _, width = spectrum_ref.shape
     spectrum = jnp.concatenate([spectrum_ref[piece] for piece in range(pieces)], axis=1)
-    columns = [blocks_ref[:, piece_columns(piece, core, width)] for piece in range(pieces)]
+    columns = [blocks_ref[:, mixed_columns(piece, core, width)] for piece in range(pieces)]
     return dot(jnp.concatenate(columns, axis=1), spectrum, ((1,), (1,)))
 
 
 def own_forward_kernel(spectrum_ref, blocks_ref, out_ref):
-    out_ref[...] = half_forward(spectrum_ref, blocks_ref, own_core())
+    out_ref[...] = half_forward(spectrum_ref, blocks_ref, own_mix())
 
 
 def other_forward_kernel(sensors, num_freq, spectrum_ref, own_ref, blocks_ref, out_ref):
     lanes = blocks_ref.shape[0]
-    total = (own_ref[...] + half_forward(spectrum_ref, blocks_ref, 1 - own_core())).T
+    total = (own_ref[...] + half_forward(spectrum_ref, blocks_ref, 1 - own_mix())).T
     own = own_frequency(num_freq, lanes)
     by_real = jnp.sum(jnp.where(own, total[:num_freq], 0.0), axis=0, keepdims=True)
     by_imag = jnp.sum(jnp.where(own, total[num_freq:], 0.0), axis=0, keepdims=True)
@@ -236,6 +247,7 @@
     busy = pl.CostEstimate(flops=20 * 10**9, bytes_accessed=64 << 20, transcendentals=0)
     half = pieces // 2
     cores = [[2 * place + core for place in PLACES] for core in range(2)]
+    mixes = [[2 * place + (mix ^ (place % 2)) for place in PLACES] for mix in range(2)]
     swap = [(device, device ^ 1) for device in range(pieces)]
 
     copies, table, weight = call(
@@ -246,7 +258,7 @@
         [pltpu.VMEM(x.shape, x.dtype) for x in small] + [pltpu.SemaphoreType.DMA((len(small),))],
         busy,
     )
-    spectrum = lax.all_to_all(copies, "sensor", 0, 0, axis_index_groups=cores)
+    spectrum = lax.all_to_all(copies, "sensor", 0, 0, axis_index_groups=mixes)
     other_spectrum = lax.ppermute(spectrum, "sensor", swap)
     (own,) = call(own_forward_kernel, [((lanes, rows), F32)], (spectrum, blocks), cost=busy)
     (partial,) = call(

time: 49.7 us -> 49.6 us (level)
  starting transfers between devices: 18 us -> 16.4 us
  blocking collectives: 19.4 us -> 20.9 us
    ppermute x1, starting transfers between devices: 2.09 us -> 0.01 us  [per_device(): other_spectrum = lax.ppermute(spectrum, 'sensor', swap)]
    all_to_all x1, blocking collectives: 11.6 us -> 12.8 us  [per_device(): spectrum = lax.all_to_all(copies, 'sensor', 0, 0, axis_index_groups=mixes)]
    ppermute x1, starting transfers between devices: 4.28 us -> 4.78 us  [per_device(): arrived = lax.ppermute(to_other, 'sensor', swap)]
where the time goes in v6:
time: 49.6 us; the launch traced here: 49.2 us
  blocking collectives  20.9 us (42%)
  starting transfers between devices  16.4 us (33%)
  Pallas kernels  7.75 us (16%)
  waiting for transfers between devices  4.19 us (8%)
    all_to_all x1, blocking collectives, per_device(): spectrum = lax.all_to_all(copies, 'sensor', 0, 0, axis_index_groups=mixes)  12.8 us
    ppermute x4, starting transfers between devices, partners(): lax.ppermute(value, 'param', [(i, i ^ bit) for i in range(count)])  11.6 us
    all_to_all x1, blocking collectives, per_device(): adjoint = lax.all_to_all(joined, 'sensor', 0, 0, axis_index_groups=cores)  8.09 us
    pallas_call x10, Pallas kernels, call(): pl.pallas_call(kernel, out_shape=[jax.ShapeDtypeStruct(shape, dtype) for...  7.75 us
    ppermute x1, starting transfers between devices, per_device(): arrived = lax.ppermute(to_other, 'sensor', swap)  4.78 us
    ppermute x4, waiting for transfers between devices, partners(): lax.ppermute(value, 'param', [(i, i ^ bit) for i in range(count)])  4.19 us
  transfers between devices with their start and end apart: 6, of which 4 were waited for; matrix products, arithmetic and copies ran while one was open for 0% of the time, Pallas kernels for 5%

profile of v6, /device:TPU:1, one launch (start us, length us, event | category | flops | bytes accessed | tf_op | source)
XLA Modules:
  0.0 49.2 jit_solution(7311000724090374013)
XLA Ops:
  0.0 0.0 copy-start
  0.0 1.5 %shard_map.55 = (bf16[8,32,256]{2,1,0:T(8,128)(2,1)S(1)}, bf16[96,420]{1,0:T(8,128)(2,1)S(1)}, f32[1,1280]{1,0:T(1,128)S(1)}) custom-call(s32[1,16]{1,0:T(1,128)} %bitcast.9, f32[420,256]{1,0:T(8,128)} %motion_hbm.1, s32[1,40]{1,0:T(1,128)} %bitcast.10, f32[5,128]{1,0:T(8,128)} %bitcast.8), custom_call_target="tpu_custom_call" | custom-call | flops 20000000000 | bytes 67108864 | tf_op jit(solution)/shard_map/pallas_call | solution.py:227
  1.5 12.8 %all_to_all.10.spectrum_ref = bf16[8,32,256]{2,1,0:T(8,128)(2,1)S(1)} all-to-all(bf16[8,32,256]{2,1,0:T(8,128)(2,1)S(1)} %get-tuple-element.12), channel_id=1, replica_groups={{0,11,4,15,8,3,12,7},{1,10,5,14,9,2,13,6},{16,27,20,31,24,19,28,23},{17..., dimensions={0} | all-to-all | bytes 262144 | tf_op jit(solution)/shard_map/all_to_all | solution.py:261
  14.3 0.0 collective-permute-start
  14.3 0.0 copy-done
  14.3 1.5 %shard_map.56.own_ref = f32[1280,32]{1,0:T(8,128)S(1)} custom-call(bf16[8,32,256]{2,1,0:T(8,128)(2,1)S(1)} %all_to_all.10.spectrum_ref, bf16[1280,4096]{1,0:T(8,128)(2,1)S(1)} %bitcast.4), custom_call_target="tpu_custom_call" | custom-call | flops 20000000000 | bytes 67108864 | tf_op jit(solution)/shard_map/pallas_call | solution.py:227
  15.8 0.0 collective-permute-done.spectrum_ref
  15.8 1.6 %shard_map.57.own_ref = f32[1,1280]{1,0:T(1,128)S(1)} custom-call(bf16[8,32,256]{2,1,0:T(8,128)(2,1)S(1)} %collective-permute-done.spectrum_ref, f32[1280,32]{1,0:T(8,128)S(1)} %shard_map.56.own_ref, bf16[1280,4096]{1,0:T(8,128)(2,1)S(1)} %bitcast.5), custom_call_target="tpu_custom_call" | custom-call | flops 20000000000 | bytes 67108864 | tf_op jit(solution)/shard_map/pallas_call | solution.py:227
  17.4 1.4 %collective-permute-start.1 = (f32[1,1280]{1,0:T(1,128)S(1)}, f32[1,1280]{1,0:T(1,128)S(1)}, u32[]{:S(2)}, u32[]{:S(2)}) collective-permute-start(f32[1,1280]{1,0:T(1,128)S(1)} %shard_map.57.own_ref), channel_id=1, source_target_pairs={{0,16},{16,0},{32,48},{48,32},{64,80},{80,64},{96,112},{112,96},{1... | collective-permute-start | bytes 15368 | tf_op jit(solution)/shard_map/ppermute | solution.py:274
  18.8 1.2 %collective-permute-done.1.refs_0_ = f32[1,1280]{1,0:T(1,128)S(1)} collective-permute-done((f32[1,1280]{1,0:T(1,128)S(1)}, f32[1,1280]{1,0:T(1,128)S(1)}, u32[]{:S(2)}, u32[]{:S(2)}) %collective-permute-start.1) | collective-permute-done | bytes 5152 | tf_op jit(solution)/shard_map/ppermute | solution.py:274
  20.0 2.7 %collective-permute-start.2 = (f32[1,1280]{1,0:T(1,128)S(1)}, f32[1,1280]{1,0:T(1,128)S(1)}, u32[]{:S(2)}, u32[]{:S(2)}) collective-permute-start(f32[1,1280]{1,0:T(1,128)S(1)} %shard_map.58.own_ref), channel_id=1, source_target_pairs={{0,48},{16,32},{32,16},{48,0},{64,112},{80,96},{96,80},{112,64},{1... | collective-permute-start | bytes 15368 | tf_op jit(solution)/shard_map/ppermute | solution.py:274
  22.7 1.0 %collective-permute-done.2.refs_0_ = f32[1,1280]{1,0:T(1,128)S(1)} collective-permute-done((f32[1,1280]{1,0:T(1,128)S(1)}, f32[1,1280]{1,0:T(1,128)S(1)}, u32[]{:S(2)}, u32[]{:S(2)}) %collective-permute-start.2) | collective-permute-done | bytes 5152 | tf_op jit(solution)/shard_map/ppermute | solution.py:274
  23.7 3.0 %collective-permute-start.3 = (f32[1,1280]{1,0:T(1,128)S(1)}, f32[1,1280]{1,0:T(1,128)S(1)}, u32[]{:S(2)}, u32[]{:S(2)}) collective-permute-start(f32[1,1280]{1,0:T(1,128)S(1)} %shard_map.59.own_ref), channel_id=1, source_target_pairs={{0,64},{16,80},{32,96},{48,112},{64,0},{80,16},{96,32},{112,48},{1... | collective-permute-start | bytes 15368 | tf_op jit(solution)/shard_map/ppermute | solution.py:274
  26.7 1.0 %collective-permute-done.3.refs_0_ = f32[1,1280]{1,0:T(1,128)S(1)} collective-permute-done((f32[1,1280]{1,0:T(1,128)S(1)}, f32[1,1280]{1,0:T(1,128)S(1)}, u32[]{:S(2)}, u32[]{:S(2)}) %collective-permute-start.3) | collective-permute-done | bytes 5152 | tf_op jit(solution)/shard_map/ppermute | solution.py:274
  27.7 4.5 %collective-permute-start.4 = (f32[1,1280]{1,0:T(1,128)S(1)}, f32[1,1280]{1,0:T(1,128)S(1)}, u32[]{:S(2)}, u32[]{:S(2)}) collective-permute-start(f32[1,1280]{1,0:T(1,128)S(1)} %shard_map.60.refs_0_), channel_id=1, source_target_pairs={{0,192},{16,208},{32,224},{48,240},{64,128},{80,144},{96,160},{112... | collective-permute-start | bytes 15368 | tf_op jit(solution)/shard_map/ppermute | solution.py:274
  32.2 1.0 %collective-permute-done.4.refs_1_ = f32[1,1280]{1,0:T(1,128)S(1)} collective-permute-done((f32[1,1280]{1,0:T(1,128)S(1)}, f32[1,1280]{1,0:T(1,128)S(1)}, u32[]{:S(2)}, u32[]{:S(2)}) %collective-permute-start.4) | collective-permute-done | bytes 5152 | tf_op jit(solution)/shard_map/ppermute | solution.py:274
  33.2 1.0 %shard_map.61 = (bf16[8,32,256]{2,1,0:T(8,128)(2,1)S(1)}, bf16[32,1280]{1,0:T(8,128)(2,1)S(1)}) custom-call(f32[1,1280]{1,0:T(1,128)S(1)} %get-tuple-element.11.weight_ref, bf16[1280,4096]{1,0:T(8,128)(2,1)S(1)} %bitcast.6, f32[1,1280]{1,0:T(1,128)S(1)} %shard_map.60.refs_0_, f32[1,1280]{1,0:T(1,128)S(1)} %collective-permute-done.4.refs_1_), custom_call_target="tpu_custom_call" | custom-call | flops 20000000000 | bytes 67108864 | tf_op jit(solution)/shard_map/pallas_call | solution.py:227
  34.2 4.8 %collective-permute-start.5 = (bf16[8,32,256]{2,1,0:T(8,128)(2,1)S(1)}, bf16[8,32,256]{2,1,0:T(8,128)(2,1)S(1)}, u32[]{:S(2)}, u32[]{:S(2)}) collective-permute-start(bf16[8,32,256]{2,1,0:T(8,128)(2,1)S(1)} %get-tuple-element.14), channel_id=1, source_target_pairs={{0,1},{1,0},{2,3},{3,2},{4,5},{5,4},{6,7},{7,6},{8,9},{9,8},{10,11... | collective-permute-start | bytes 393224 | tf_op jit(solution)/shard_map/ppermute | solution.py:285
  39.0 1.0 %shard_map.62.first_ref = f32[8,32,256]{2,1,0:T(8,128)S(1)} custom-call(bf16[32,1280]{1,0:T(8,128)(2,1)S(1)} %get-tuple-element.13.left_ref, bf16[1280,4096]{1,0:T(8,128)(2,1)S(1)} %bitcast.7), custom_call_target="tpu_custom_call" | custom-call | flops 20000000000 | bytes 67108864 | tf_op jit(solution)/shard_map/pallas_call | solution.py:227
  40.1 0.0 collective-permute-done.5.arrived_ref
  40.1 8.1 %all_to_all.11.adjoint_ref = bf16[8,32,256]{2,1,0:T(8,128)(2,1)S(1)} all-to-all(bf16[8,32,256]{2,1,0:T(8,128)(2,1)S(1)} %shard_map.63), channel_id=1, replica_groups={{0,10,4,14,8,2,12,6},{1,11,5,15,9,3,13,7},{16,26,20,30,24,18,28,22},{17..., dimensions={0} | all-to-all | bytes 262144 | tf_op jit(solution)/shard_map/all_to_all | solution.py:288
  48.2 1.0 %shard_map.64 = f32[420,256]{1,0:T(8,128)} custom-call(bf16[96,420]{1,0:T(8,128)(2,1)S(1)} %get-tuple-element.10.table_ref, bf16[8,32,256]{2,1,0:T(8,128)(2,1)S(1)} %all_to_all.11.adjoint_ref), custom_call_target="tpu_custom_call" | custom-call | tf_op jit(solution)/shard_map/pallas_call | solution.py:227
  (4 shorter events, 0.0 us)
Async XLA Ops:
  0.0 14.3 %copy-start = (bf16[16,2,40,4096]{3,2,1,0:T(8,128)(2,1)S(1)}, bf16[16,2,40,4096]{3,2,1,0:T(8,128)(2,1)}, u32[]{:S(2)}) copy-start(bf16[16,2,40,4096]{3,2,1,0:T(8,128)(2,1)} %param.6) | copy-start | bytes 31457284
  14.3 1.5 %collective-permute-start = (bf16[8,32,256]{2,1,0:T(8,128)(2,1)S(1)}, bf16[8,32,256]{2,1,0:T(8,128)(2,1)S(1)}, u32[]{:S(2)}, u32[]{:S(2)}) collective-permute-start(bf16[8,32,256]{2,1,0:T(8,128)(2,1)S(1)} %all_to_all.10.spectrum_ref), channel_id=1, source_target_pairs={{0,1},{1,0},{2,3},{3,2},{4,5},{5,4},{6,7},{7,6},{8,9},{9,8},{10,11... | collective-permute-start | bytes 393224 | tf_op jit(solution)/shard_map/ppermute | solution.py:262
  17.4 2.6 %collective-permute-start.1 = (f32[1,1280]{1,0:T(1,128)S(1)}, f32[1,1280]{1,0:T(1,128)S(1)}, u32[]{:S(2)}, u32[]{:S(2)}) collective-permute-start(f32[1,1280]{1,0:T(1,128)S(1)} %shard_map.57.own_ref), channel_id=1, source_target_pairs={{0,16},{16,0},{32,48},{48,32},{64,80},{80,64},{96,112},{112,96},{1... | collective-permute-start | bytes 15368 | tf_op jit(solution)/shard_map/ppermute | solution.py:274
  20.0 3.7 %collective-permute-start.2 = (f32[1,1280]{1,0:T(1,128)S(1)}, f32[1,1280]{1,0:T(1,128)S(1)}, u32[]{:S(2)}, u32[]{:S(2)}) collective-permute-start(f32[1,1280]{1,0:T(1,128)S(1)} %shard_map.58.own_ref), channel_id=1, source_target_pairs={{0,48},{16,32},{32,16},{48,0},{64,112},{80,96},{96,80},{112,64},{1... | collective-permute-start | bytes 15368 | tf_op jit(solution)/shard_map/ppermute | solution.py:274
  23.7 4.0 %collective-permute-start.3 = (f32[1,1280]{1,0:T(1,128)S(1)}, f32[1,1280]{1,0:T(1,128)S(1)}, u32[]{:S(2)}, u32[]{:S(2)}) collective-permute-start(f32[1,1280]{1,0:T(1,128)S(1)} %shard_map.59.own_ref), channel_id=1, source_target_pairs={{0,64},{16,80},{32,96},{48,112},{64,0},{80,16},{96,32},{112,48},{1... | collective-permute-start | bytes 15368 | tf_op jit(solution)/shard_map/ppermute | solution.py:274
  27.7 5.5 %collective-permute-start.4 = (f32[1,1280]{1,0:T(1,128)S(1)}, f32[1,1280]{1,0:T(1,128)S(1)}, u32[]{:S(2)}, u32[]{:S(2)}) collective-permute-start(f32[1,1280]{1,0:T(1,128)S(1)} %shard_map.60.refs_0_), channel_id=1, source_target_pairs={{0,192},{16,208},{32,224},{48,240},{64,128},{80,144},{96,160},{112... | collective-permute-start | bytes 15368 | tf_op jit(solution)/shard_map/ppermute | solution.py:274
  34.2 5.8 %collective-permute-start.5 = (bf16[8,32,256]{2,1,0:T(8,128)(2,1)S(1)}, bf16[8,32,256]{2,1,0:T(8,128)(2,1)S(1)}, u32[]{:S(2)}, u32[]{:S(2)}) collective-permute-start(bf16[8,32,256]{2,1,0:T(8,128)(2,1)S(1)} %get-tuple-element.14), channel_id=1, source_target_pairs={{0,1},{1,0},{2,3},{3,2},{4,5},{5,4},{6,7},{7,6},{8,9},{9,8},{10,11... | collective-permute-start | bytes 393224 | tf_op jit(solution)/shard_map/ppermute | solution.py:285

commit v7 on v5

--- a/solution.py
+++ b/solution.py
@@ -9,7 +9,7 @@
 from jax.sharding import PartitionSpec as P
 
 F32 = jnp.float32
-STAGES = ((1,), (3,), (4,), (12,))
+STAGES = ((1,), (3,), (12,), (4,))
 PLACES = (0, 5, 2, 7, 4, 1, 6, 3)
 BF16 = jnp.bfloat16
 VMEM = pl.BlockSpec(memory_space=pltpu.VMEM)

time: 49.7 us -> 49.7 us (level)
  starting transfers between devices: 18 us -> 17 us
  waiting for transfers between devices: 4.19 us -> 5.14 us
    ppermute x4, waiting for transfers between devices: 4.19 us -> 5.14 us  [partners(): lax.ppermute(value, 'param', [(i, i ^ bit) for i in range(count)])]
    ppermute x4, starting transfers between devices: 11.6 us -> 10.7 us  [partners(): lax.ppermute(value, 'param', [(i, i ^ bit) for i in range(count)])]
where the time goes in v7:
time: 49.7 us; the launch traced here: 49.3 us
  blocking collectives  19.4 us (39%)
  starting transfers between devices  17 us (34%)
  Pallas kernels  7.74 us (16%)
  waiting for transfers between devices  5.14 us (10%)
    all_to_all x1, blocking collectives, per_device(): spectrum = lax.all_to_all(copies, 'sensor', 0, 0, axis_index_groups=cores)  11.6 us
    ppermute x4, starting transfers between devices, partners(): lax.ppermute(value, 'param', [(i, i ^ bit) for i in range(count)])  10.7 us
    all_to_all x1, blocking collectives, per_device(): adjoint = lax.all_to_all(joined, 'sensor', 0, 0, axis_index_groups=cores)  7.75 us
    pallas_call x10, Pallas kernels, call(): pl.pallas_call(kernel, out_shape=[jax.ShapeDtypeStruct(shape, dtype) for...  7.74 us
    ppermute x4, waiting for transfers between devices, partners(): lax.ppermute(value, 'param', [(i, i ^ bit) for i in range(count)])  5.14 us
    ppermute x1, starting transfers between devices, per_device(): arrived = lax.ppermute(to_other, 'sensor', swap)  4.25 us
    ppermute x1, starting transfers between devices, per_device(): other_spectrum = lax.ppermute(spectrum, 'sensor', swap)  2.09 us
  transfers between devices with their start and end apart: 6, of which 4 were waited for; matrix products, arithmetic and copies ran while one was open for 0% of the time, Pallas kernels for 5%

profile of v7, /device:TPU:1, one launch (start us, length us, event | category | flops | bytes accessed | tf_op | source)
XLA Modules:
  0.0 49.3 jit_solution(15510970798447438777)
XLA Ops:
  0.0 0.0 copy-start
  0.0 1.5 %shard_map.55 = (bf16[8,32,256]{2,1,0:T(8,128)(2,1)S(1)}, bf16[96,420]{1,0:T(8,128)(2,1)S(1)}, f32[1,1280]{1,0:T(1,128)S(1)}) custom-call(s32[1,16]{1,0:T(1,128)} %bitcast.9, f32[420,256]{1,0:T(8,128)} %motion_hbm.1, s32[1,40]{1,0:T(1,128)} %bitcast.10, f32[5,128]{1,0:T(8,128)} %bitcast.8), custom_call_target="tpu_custom_call" | custom-call | flops 20000000000 | bytes 67108864 | tf_op jit(solution)/shard_map/pallas_call | solution.py:216
  1.5 11.6 %all_to_all.10.spectrum_ref = bf16[8,32,256]{2,1,0:T(8,128)(2,1)S(1)} all-to-all(bf16[8,32,256]{2,1,0:T(8,128)(2,1)S(1)} %get-tuple-element.12), channel_id=1, replica_groups={{0,10,4,14,8,2,12,6},{1,11,5,15,9,3,13,7},{16,26,20,30,24,18,28,22},{17..., dimensions={0} | all-to-all | bytes 262144 | tf_op jit(solution)/shard_map/all_to_all | solution.py:249
  13.1 2.1 %collective-permute-start = (bf16[8,32,256]{2,1,0:T(8,128)(2,1)S(1)}, bf16[8,32,256]{2,1,0:T(8,128)(2,1)S(1)}, u32[]{:S(2)}, u32[]{:S(2)}) collective-permute-start(bf16[8,32,256]{2,1,0:T(8,128)(2,1)S(1)} %all_to_all.10.spectrum_ref), channel_id=1, source_target_pairs={{0,1},{1,0},{2,3},{3,2},{4,5},{5,4},{6,7},{7,6},{8,9},{9,8},{10,11... | collective-permute-start | bytes 393224 | tf_op jit(solution)/shard_map/ppermute | solution.py:250
  15.2 0.0 copy-done
  15.2 1.5 %shard_map.56.own_ref = f32[1280,32]{1,0:T(8,128)S(1)} custom-call(bf16[8,32,256]{2,1,0:T(8,128)(2,1)S(1)} %all_to_all.10.spectrum_ref, bf16[1280,4096]{1,0:T(8,128)(2,1)S(1)} %bitcast.4), custom_call_target="tpu_custom_call" | custom-call | flops 20000000000 | bytes 67108864 | tf_op jit(solution)/shard_map/pallas_call | solution.py:216
  16.7 0.0 collective-permute-done.spectrum_ref
  16.8 1.6 %shard_map.57.own_ref = f32[1,1280]{1,0:T(1,128)S(1)} custom-call(bf16[8,32,256]{2,1,0:T(8,128)(2,1)S(1)} %collective-permute-done.spectrum_ref, f32[1280,32]{1,0:T(8,128)S(1)} %shard_map.56.own_ref, bf16[1280,4096]{1,0:T(8,128)(2,1)S(1)} %bitcast.5), custom_call_target="tpu_custom_call" | custom-call | flops 20000000000 | bytes 67108864 | tf_op jit(solution)/shard_map/pallas_call | solution.py:216
  18.4 1.4 %collective-permute-start.1 = (f32[1,1280]{1,0:T(1,128)S(1)}, f32[1,1280]{1,0:T(1,128)S(1)}, u32[]{:S(2)}, u32[]{:S(2)}) collective-permute-start(f32[1,1280]{1,0:T(1,128)S(1)} %shard_map.57.own_ref), channel_id=1, source_target_pairs={{0,16},{16,0},{32,48},{48,32},{64,80},{80,64},{96,112},{112,96},{1... | collective-permute-start | bytes 15368 | tf_op jit(solution)/shard_map/ppermute | solution.py:262
  19.8 1.2 %collective-permute-done.1.refs_0_ = f32[1,1280]{1,0:T(1,128)S(1)} collective-permute-done((f32[1,1280]{1,0:T(1,128)S(1)}, f32[1,1280]{1,0:T(1,128)S(1)}, u32[]{:S(2)}, u32[]{:S(2)}) %collective-permute-start.1) | collective-permute-done | bytes 5152 | tf_op jit(solution)/shard_map/ppermute | solution.py:262
  21.0 2.7 %collective-permute-start.2 = (f32[1,1280]{1,0:T(1,128)S(1)}, f32[1,1280]{1,0:T(1,128)S(1)}, u32[]{:S(2)}, u32[]{:S(2)}) collective-permute-start(f32[1,1280]{1,0:T(1,128)S(1)} %shard_map.58.own_ref), channel_id=1, source_target_pairs={{0,48},{16,32},{32,16},{48,0},{64,112},{80,96},{96,80},{112,64},{1... | collective-permute-start | bytes 15368 | tf_op jit(solution)/shard_map/ppermute | solution.py:262
  23.7 1.0 %collective-permute-done.2.refs_0_ = f32[1,1280]{1,0:T(1,128)S(1)} collective-permute-done((f32[1,1280]{1,0:T(1,128)S(1)}, f32[1,1280]{1,0:T(1,128)S(1)}, u32[]{:S(2)}, u32[]{:S(2)}) %collective-permute-start.2) | collective-permute-done | bytes 5152 | tf_op jit(solution)/shard_map/ppermute | solution.py:262
  24.7 5.1 %collective-permute-start.3 = (f32[1,1280]{1,0:T(1,128)S(1)}, f32[1,1280]{1,0:T(1,128)S(1)}, u32[]{:S(2)}, u32[]{:S(2)}) collective-permute-start(f32[1,1280]{1,0:T(1,128)S(1)} %shard_map.59.own_ref), channel_id=1, source_target_pairs={{0,192},{16,208},{32,224},{48,240},{64,128},{80,144},{96,160},{112... | collective-permute-start | bytes 15368 | tf_op jit(solution)/shard_map/ppermute | solution.py:262
  29.8 1.0 %collective-permute-done.3.refs_0_ = f32[1,1280]{1,0:T(1,128)S(1)} collective-permute-done((f32[1,1280]{1,0:T(1,128)S(1)}, f32[1,1280]{1,0:T(1,128)S(1)}, u32[]{:S(2)}, u32[]{:S(2)}) %collective-permute-start.3) | collective-permute-done | bytes 5152 | tf_op jit(solution)/shard_map/ppermute | solution.py:262
  30.8 1.4 %collective-permute-start.4 = (f32[1,1280]{1,0:T(1,128)S(1)}, f32[1,1280]{1,0:T(1,128)S(1)}, u32[]{:S(2)}, u32[]{:S(2)}) collective-permute-start(f32[1,1280]{1,0:T(1,128)S(1)} %shard_map.60.refs_0_), channel_id=1, source_target_pairs={{0,64},{16,80},{32,96},{48,112},{64,0},{80,16},{96,32},{112,48},{1... | collective-permute-start | bytes 15368 | tf_op jit(solution)/shard_map/ppermute | solution.py:262
  32.3 2.0 %collective-permute-done.4.refs_1_ = f32[1,1280]{1,0:T(1,128)S(1)} collective-permute-done((f32[1,1280]{1,0:T(1,128)S(1)}, f32[1,1280]{1,0:T(1,128)S(1)}, u32[]{:S(2)}, u32[]{:S(2)}) %collective-permute-start.4) | collective-permute-done | bytes 5152 | tf_op jit(solution)/shard_map/ppermute | solution.py:262
  34.2 1.0 %shard_map.61 = (bf16[8,32,256]{2,1,0:T(8,128)(2,1)S(1)}, bf16[32,1280]{1,0:T(8,128)(2,1)S(1)}) custom-call(f32[1,1280]{1,0:T(1,128)S(1)} %get-tuple-element.11.weight_ref, bf16[1280,4096]{1,0:T(8,128)(2,1)S(1)} %bitcast.6, f32[1,1280]{1,0:T(1,128)S(1)} %shard_map.60.refs_0_, f32[1,1280]{1,0:T(1,128)S(1)} %collective-permute-done.4.refs_1_), custom_call_target="tpu_custom_call" | custom-call | flops 20000000000 | bytes 67108864 | tf_op jit(solution)/shard_map/pallas_call | solution.py:216
  35.2 4.3 %collective-permute-start.5 = (bf16[8,32,256]{2,1,0:T(8,128)(2,1)S(1)}, bf16[8,32,256]{2,1,0:T(8,128)(2,1)S(1)}, u32[]{:S(2)}, u32[]{:S(2)}) collective-permute-start(bf16[8,32,256]{2,1,0:T(8,128)(2,1)S(1)} %get-tuple-element.14), channel_id=1, source_target_pairs={{0,1},{1,0},{2,3},{3,2},{4,5},{5,4},{6,7},{7,6},{8,9},{9,8},{10,11... | collective-permute-start | bytes 393224 | tf_op jit(solution)/shard_map/ppermute | solution.py:273
  39.5 1.0 %shard_map.62.first_ref = f32[8,32,256]{2,1,0:T(8,128)S(1)} custom-call(bf16[32,1280]{1,0:T(8,128)(2,1)S(1)} %get-tuple-element.13.left_ref, bf16[1280,4096]{1,0:T(8,128)(2,1)S(1)} %bitcast.7), custom_call_target="tpu_custom_call" | custom-call | flops 20000000000 | bytes 67108864 | tf_op jit(solution)/shard_map/pallas_call | solution.py:216
  40.5 0.0 collective-permute-done.5.arrived_ref
  40.6 7.7 %all_to_all.11.adjoint_ref = bf16[8,32,256]{2,1,0:T(8,128)(2,1)S(1)} all-to-all(bf16[8,32,256]{2,1,0:T(8,128)(2,1)S(1)} %shard_map.63), channel_id=1, replica_groups={{0,10,4,14,8,2,12,6},{1,11,5,15,9,3,13,7},{16,26,20,30,24,18,28,22},{17..., dimensions={0} | all-to-all | bytes 262144 | tf_op jit(solution)/shard_map/all_to_all | solution.py:276
  48.3 1.0 %shard_map.64 = f32[420,256]{1,0:T(8,128)} custom-call(bf16[96,420]{1,0:T(8,128)(2,1)S(1)} %get-tuple-element.10.table_ref, bf16[8,32,256]{2,1,0:T(8,128)(2,1)S(1)} %all_to_all.11.adjoint_ref), custom_call_target="tpu_custom_call" | custom-call | tf_op jit(solution)/shard_map/pallas_call | solution.py:216
  (4 shorter events, 0.0 us)
Async XLA Ops:
  0.0 15.2 %copy-start = (bf16[16,2,40,4096]{3,2,1,0:T(8,128)(2,1)S(1)}, bf16[16,2,40,4096]{3,2,1,0:T(8,128)(2,1)}, u32[]{:S(2)}) copy-start(bf16[16,2,40,4096]{3,2,1,0:T(8,128)(2,1)} %param.6) | copy-start | bytes 31457284
  13.1 3.6 %collective-permute-start = (bf16[8,32,256]{2,1,0:T(8,128)(2,1)S(1)}, bf16[8,32,256]{2,1,0:T(8,128)(2,1)S(1)}, u32[]{:S(2)}, u32[]{:S(2)}) collective-permute-start(bf16[8,32,256]{2,1,0:T(8,128)(2,1)S(1)} %all_to_all.10.spectrum_ref), channel_id=1, source_target_pairs={{0,1},{1,0},{2,3},{3,2},{4,5},{5,4},{6,7},{7,6},{8,9},{9,8},{10,11... | collective-permute-start | bytes 393224 | tf_op jit(solution)/shard_map/ppermute | solution.py:250
  18.4 2.6 %collective-permute-start.1 = (f32[1,1280]{1,0:T(1,128)S(1)}, f32[1,1280]{1,0:T(1,128)S(1)}, u32[]{:S(2)}, u32[]{:S(2)}) collective-permute-start(f32[1,1280]{1,0:T(1,128)S(1)} %shard_map.57.own_ref), channel_id=1, source_target_pairs={{0,16},{16,0},{32,48},{48,32},{64,80},{80,64},{96,112},{112,96},{1... | collective-permute-start | bytes 15368 | tf_op jit(solution)/shard_map/ppermute | solution.py:262
  21.0 3.7 %collective-permute-start.2 = (f32[1,1280]{1,0:T(1,128)S(1)}, f32[1,1280]{1,0:T(1,128)S(1)}, u32[]{:S(2)}, u32[]{:S(2)}) collective-permute-start(f32[1,1280]{1,0:T(1,128)S(1)} %shard_map.58.own_ref), channel_id=1, source_target_pairs={{0,48},{16,32},{32,16},{48,0},{64,112},{80,96},{96,80},{112,64},{1... | collective-permute-start | bytes 15368 | tf_op jit(solution)/shard_map/ppermute | solution.py:262
  24.7 6.1 %collective-permute-start.3 = (f32[1,1280]{1,0:T(1,128)S(1)}, f32[1,1280]{1,0:T(1,128)S(1)}, u32[]{:S(2)}, u32[]{:S(2)}) collective-permute-start(f32[1,1280]{1,0:T(1,128)S(1)} %shard_map.59.own_ref), channel_id=1, source_target_pairs={{0,192},{16,208},{32,224},{48,240},{64,128},{80,144},{96,160},{112... | collective-permute-start | bytes 15368 | tf_op jit(solution)/shard_map/ppermute | solution.py:262
  30.8 3.4 %collective-permute-start.4 = (f32[1,1280]{1,0:T(1,128)S(1)}, f32[1,1280]{1,0:T(1,128)S(1)}, u32[]{:S(2)}, u32[]{:S(2)}) collective-permute-start(f32[1,1280]{1,0:T(1,128)S(1)} %shard_map.60.refs_0_), channel_id=1, source_target_pairs={{0,64},{16,80},{32,96},{48,112},{64,0},{80,16},{96,32},{112,48},{1... | collective-permute-start | bytes 15368 | tf_op jit(solution)/shard_map/ppermute | solution.py:262
  35.2 5.3 %collective-permute-start.5 = (bf16[8,32,256]{2,1,0:T(8,128)(2,1)S(1)}, bf16[8,32,256]{2,1,0:T(8,128)(2,1)S(1)}, u32[]{:S(2)}, u32[]{:S(2)}) collective-permute-start(bf16[8,32,256]{2,1,0:T(8,128)(2,1)S(1)} %get-tuple-element.14), channel_id=1, source_target_pairs={{0,1},{1,0},{2,3},{3,2},{4,5},{5,4},{6,7},{7,6},{8,9},{9,8},{10,11... | collective-permute-start | bytes 393224 | tf_op jit(solution)/shard_map/ppermute | solution.py:273
